TPU v7x, 128 devices: a whole 4x4x4 slice. The times are simulated.
128 devices in a mesh: rep: 8 (over z, y_hi), shard: 16 (over y_lo, x, core).
Axes of the slice: x: 4, y: 4 (y_hi: 2, y_lo: 2; y = y_hi * 2 + y_lo), z: 4, core: 2. Of those that a mesh axis runs over, the one named last changes fastest.
Arguments:
- tokens: bfloat16 [65536, 4096], P(('rep', 'shard')), may hold values from -24 to 24
- hidden_grad: bfloat16 [65536, 896], P(('rep', 'shard')), may hold values from -6 to 6
- master: float32 [4096, 1792], P('shard'), may hold values from -6 to 6
- moment_first: float32 [4096, 1792], P('shard'), may hold values from -6 to 6
- moment_second: float32 [4096, 1792], P('shard'), may hold values from 0.5 to 8
Outputs:
- input_grad: bfloat16 [65536, 4096], P(('rep', 'shard'))
- master_next: float32 [4096, 1792], P('shard')
- first_next: float32 [4096, 1792], P('shard')
- second_next: float32 [4096, 1792], P('shard')
All inputs are finite; a program needn't handle non-finite values.
Results may differ from a plain program's by a relative error of at most 0.029.
Values may be sent and summed in bfloat16 or wider, within the bound.
A program may use at most 128 MiB of HBM per device.

v0:
```python
import jax
import jax.numpy as jnp
from jax import lax
from jax.sharding import PartitionSpec as P

bias_first = 0.999973438601
bias_second = 0.99407947078


def adamw(master, moment_first, moment_second, grad):
    first_next = 0.9 * moment_first + 0.1 * grad
    second_next = 0.95 * moment_second + 0.05 * grad * grad
    corrected_one = first_next / bias_first
    corrected_two = second_next / bias_second
    update = corrected_one / (jnp.sqrt(corrected_two) + 1e-08) + 0.1 * master
    return (master - 0.01 * update, first_next, second_next)


def contract_rows(left, right):
    return lax.dot_general(
        left, right, (((0,), (0,)), ((), ())), preferred_element_type=jnp.float32
    )


def contract_cols(left, right):
    return lax.dot_general(
        left, right, (((1,), (1,)), ((), ())), preferred_element_type=jnp.float32
    )


def body(tokens, hidden_grad, master, moment_first, moment_second):
    multiplier = tokens.shape[1] ** (-0.5)
    hidden_width = hidden_grad.shape[1]
    weights_local = master.astype(jnp.bfloat16)
    gathered = lax.all_gather(weights_local, "shard", axis=0, tiled=True)
    gate_up = jnp.dot(tokens, gathered, preferred_element_type=jnp.float32) * multiplier
    gate = gate_up[:, :hidden_width]
    upward = gate_up[:, hidden_width:]
    cotangent = hidden_grad.astype(jnp.float32)
    sigmoid_gate = jax.nn.sigmoid(gate)
    grad_gate = cotangent * upward * sigmoid_gate * (1.0 + gate * (1.0 - sigmoid_gate))
    grad_up = cotangent * gate * sigmoid_gate
    branch_grad = jnp.concatenate([grad_gate, grad_up], axis=1).astype(jnp.bfloat16)
    input_grad = contract_cols(branch_grad, gathered) * multiplier
    input_grad = input_grad.astype(jnp.bfloat16)
    grad = lax.psum_scatter(
        (contract_rows(tokens, branch_grad) * multiplier).astype(jnp.bfloat16),
        "shard",
        scatter_dimension=0,
        tiled=True,
    )
    total = lax.psum(grad, "rep").astype(jnp.float32)
    master_next, first_next, second_next = adamw(master, moment_first, moment_second, total)
    return (input_grad, master_next, first_next, second_next)


def solution(mesh):
    return jax.shard_map(
        body,
        mesh=mesh,
        in_specs=(
            P(("rep", "shard"), None),
            P(("rep", "shard"), None),
            P("shard", None),
            P("shard", None),
            P("shard", None),
        ),
        out_specs=(P(("rep", "shard"), None), P("shard", None), P("shard", None), P("shard", None)),
        check_vma=False,
    )
```

profile of v0, /device:TPU:1, one launch (start us, length us, event | category | flops | bytes accessed | tf_op | source)
XLA Modules:
  0.0 314.9 jit_solution(16748673503142851256)
XLA Ops:
  7.2 0.0 all-gather.2.cloned.1.call-start
  7.2 2.5 convert_element_type.20
  9.7 0.0 all-gather.2.cloned.1.call-update
  9.8 0.0 copy-start.4
  9.8 0.0 reduce-scatter.2.cloned.1.call-start
  9.8 85.8 %all-gather.2.cloned.1.call-done = bf16[4096,1792]{1,0:T(8,128)(2,1)} async-done(((bf16[256,1792]{1,0:T(8,128)(2,1)}), bf16[4096,1792]{1,0:T(8,128)(2,1)}) %all-gather.2.cloned.1.call-update) | async-done | bytes 14680080 | tf_op jit(solution)/shard_map/all_gather | solution.py:35
  95.7 11.9 %convolution_multiply_fusion = f32[512,1792]{1,0:T(8,128)S(1)} fusion(bf16[512,4096]{1,0:T(8,128)(2,1)} %param.5, bf16[4096,1792]{1,0:T(8,128)(2,1)} %all-gather.2.cloned.1.call-done), kind=kOutput, calls=%fused_computation.3 | convolution fusion | flops 7517110272 | bytes 22544384 | tf_op jit(solution)/shard_map/dot_general | solution.py:36
  107.6 0.0 copy-done.4
  107.6 0.0 copy-start.6
  107.6 0.9 fusion.3
  108.5 0.0 copy-start.5
  108.5 1.6 copy-done.6
  110.1 11.2 %fusion = bf16[4096,1792]{0,1:T(8,128)(2,1)} fusion(bf16[512,4096]{1,0:T(8,128)(2,1)S(1)} %copy-done.6, bf16[512,896]{1,0:T(8,128)(2,1)S(1)} %get-tuple-element.12, bf16[512,896]{1,0:T(8,128)(2,1)S(1)} %get-tuple-element.11), kind=kOutput, calls=%fused_computation.1 | convolution fusion | flops 7534542848 | bytes 20709376 | tf_op jit(solution)/shard_map/dot_general | solution.py:20
  121.3 0.0 copy-done.5
  121.4 0.0 copy-start
  121.4 0.0 reduce-scatter.2.cloned.1.call-update
  121.4 0.2 all-reduce.2.cloned.1.call-start
  121.6 1.2 copy-done
  122.9 1.7 copy.12
  124.5 0.0 copy-start.3
  124.5 2.9 copy.9
  127.4 0.0 copy-done.3
  127.4 1.7 copy.10
  129.1 79.0 %reduce-scatter.2.cloned.1.call-done = bf16[256,1792]{0,1:T(8,128)(2,1)} async-done(((bf16[4096,1792]{0,1:T(8,128)(2,1)}), bf16[256,1792]{0,1:T(8,128)(2,1)}) %reduce-scatter.2.cloned.1.call-update) | async-done | bytes 917520 | tf_op jit(solution)/shard_map/reduce_scatter | solution.py:46
  208.1 0.0 all-reduce.2.cloned.1.call-update
  208.1 0.0 copy-start.1
  208.1 12.7 %multiply_convert_fusion.1 = bf16[512,4096]{1,0:T(8,128)(2,1)} fusion(bf16[4096,1792]{1,0:T(8,128)(2,1)} %all-gather.2.cloned.1.call-done, bf16[512,896]{1,0:T(8,128)(2,1)} %copy-done.5, bf16[512,896]{1,0:T(8,128)(2,1)S(1)} %get-tuple-element.11), kind=kOutput, calls=%fused_computation.2 | convolution fusion | flops 7524057088 | bytes 20709376 | tf_op jit(solution)/shard_map/dot_general | solution.py:26
  220.9 74.6 %all-reduce.2.cloned.1.call-done = bf16[256,1792]{0,1:T(8,128)(2,1)} async-done(((bf16[256,1792]{0,1:T(8,128)(2,1)}), bf16[256,1792]{0,1:T(8,128)(2,1)}) %all-reduce.2.cloned.1.call-update) | async-done | bytes 917520 | tf_op jit(solution)/shard_map/psum | solution.py:52
  295.4 0.0 copy-done.1
  295.4 5.7 %multiply_subtract_fusion = (f32[256,1792]{0,1:T(8,128)}, f32[256,1792]{0,1:T(8,128)}, f32[256,1792]{0,1:T(8,128)}) fusion(f32[256,1792]{0,1:T(8,128)S(1)} %copy-done.1, bf16[256,1792]{0,1:T(8,128)(2,1)} %all-reduce.2.cloned.1.call-done, f32[256,1792]{0,1:T(8,128)} %copy.9, f32[256,1792]{0,1:T(8,128)} %copy.10), kind=kLoop, calls=%fused_computation.16 | loop fusion | flops 7340032 | bytes 11927552 | tf_op jit(solution)/shard_map/sub | solution.py:16
  301.1 2.7 copy.13
  303.8 0.0 copy-start.2
  303.8 2.9 copy.14
  306.7 0.0 copy-done.2
  306.7 1.7 copy.15
Async XLA Ops:
  7.2 88.5 %all-gather.2.cloned.1.call-start = ((), (), s32[]{:S(2)}) async-start(), calls=%async_computation.1 | async-start | bytes 15597568 | tf_op jit(solution)/shard_map/all_gather | solution.py:35
  9.8 97.8 %copy-start.4 = (bf16[512,896]{1,0:T(8,128)(2,1)S(1)}, bf16[512,896]{1,0:T(8,128)(2,1)}, u32[]{:S(2)}) copy-start(bf16[512,896]{1,0:T(8,128)(2,1)} %param.6) | copy-start | bytes 2752516
  9.8 198.3 %reduce-scatter.2.cloned.1.call-start = ((), (), s32[]{:S(2)}) async-start(), calls=%async_computation.2 | async-start | bytes 15597568 | tf_op jit(solution)/shard_map/reduce_scatter | solution.py:46
  107.6 2.5 copy-start.6
  108.5 12.8 %copy-start.5 = (bf16[512,896]{1,0:T(8,128)(2,1)}, bf16[512,896]{1,0:T(8,128)(2,1)S(1)}, u32[]{:S(2)}) copy-start(bf16[512,896]{1,0:T(8,128)(2,1)S(1)} %get-tuple-element.12) | copy-start | bytes 2752516
  121.4 1.5 copy-start
  121.4 174.0 %all-reduce.2.cloned.1.call-start = ((), (), s32[]{:S(2)}) async-start(), calls=%async_computation.3 | async-start | bytes 1835008 | tf_op jit(solution)/shard_map/psum | solution.py:52
  124.5 2.9 copy-start.3
  208.1 87.3 %copy-start.1 = (f32[256,1792]{0,1:T(8,128)S(1)}, f32[256,1792]{0,1:T(8,128)}, u32[]{:S(2)}) copy-start(f32[256,1792]{0,1:T(8,128)} %copy.12) | copy-start | bytes 5505028
  303.8 2.9 copy-start.2
Sparse Core Ops, SparseCore 0:
  10.3 85.3 all-gather.1
  121.5 86.5 reduce-scatter.1
  210.6 84.7 all-reduce.1
where the time goes:
time: 319 us; the launch traced here: 315 us
  waiting for transfers between devices  239 us (75%)
  matrix products  35.9 us (11%)
  local copies, waits for them, and re-layouts  16.3 us (5%)
  between operations  13.8 us (4%)
  other arithmetic  9.1 us (3%)
    all_gather x1, waiting for transfers between devices, body(): gathered = lax.all_gather(weights_local, 'shard', axis=0, tiled=True)  85.8 us
    reduce_scatter x1, waiting for transfers between devices, body(): lax.psum_scatter((contract_rows(tokens, branch_grad) * multiplier).astype...  79 us
    psum x1, waiting for transfers between devices, body(): total = lax.psum(grad, 'rep').astype(jnp.float32)  74.6 us
    unnamed x20, local copies, waits for them, and re-layouts  16.3 us
    dot_general x1, matrix products, contract_cols(): lax.dot_general(left, right, (((1,), (1,)), ((), ())), preferred_element_...  12.7 us
    dot_general x1, matrix products, body(): jnp.dot(tokens, gathered, preferred_element_type=jnp.float32) * multiplier  11.9 us
    dot_general x1, matrix products, contract_rows(): lax.dot_general(left, right, (((0,), (0,)), ((), ())), preferred_element_...  11.2 us
  transfers between devices with their start and end apart: 3, of which 3 were waited for; matrix products, arithmetic and copies ran while one was open for 6% of the time, Pallas kernels for 0%

commit v1 on v0

v1 whole, which is shorter than its diff:
```python
import jax
import jax.numpy as jnp
from jax import lax
from jax.experimental import pallas as pl
from jax.experimental.pallas import tpu as pltpu
from jax.sharding import PartitionSpec as P

MESH = pl.DeviceIdType.MESH
bias_first = 0.999973438601
bias_second = 0.99407947078
bf16, f32 = jnp.bfloat16, jnp.float32

D, FFW, TOK = 4096, 896, 512
UNIT = 512
HALF = 256
WIDTHS = (256, 256, 256, 128)
NCHUNK = len(WIDTHS)
MULT = 1.0 / 64.0
N_SEM = 160


def adamw(master, moment_first, moment_second, grad):
    first_next = 0.9 * moment_first + 0.1 * grad
    second_next = 0.95 * moment_second + 0.05 * grad * grad
    corrected_one = first_next / bias_first
    corrected_two = second_next / bias_second
    update = corrected_one / (jnp.sqrt(corrected_two) + 1e-08) + 0.1 * master
    return (master - 0.01 * update, first_next, second_next)


def add(*values):
    total = values[0].astype(f32)
    for v in values[1:]:
        total = total + v.astype(f32)
    return total


def kernel(
    tokens, hidden, master, ig_out, g_out,
    tok, tok_t, hid, mst, branch, ig_in,
    w_a, w_h, snd_a, snd_h, g_a, g_h, yr_a, yr_h, x1_a, x1_h, x2_a, x2_h,
    zr_a, zr_h, yh_a, yh_h, fin_a, fin_h, sw_a, sw_h,
    lsem, ssem, rsem,
):
    rep, shard = lax.axis_index("rep"), lax.axis_index("shard")
    z, y_hi = rep // 2, rep % 2
    y_lo, x, c = shard // 8, (shard // 2) % 4, shard % 2
    y = y_hi * 2 + y_lo
    mine = y_lo * 4 + x

    def device(dx=0, dy=0, dz=0, dc=0):
        xx, yy, zz, cc = (x + dx + 4) % 4, (y + dy + 4) % 4, (z + dz + 4) % 4, (c + dc) % 2
        return (zz * 2 + yy // 2, ((yy % 2) * 4 + xx) * 2 + cc)

    sibling = device(dc=1)
    right, left = device(dx=1), device(dx=-1)
    up, down = device(dy=1), device(dy=-1)
    far_y = device(dy=2)
    z_next = [device(dz=1), device(dz=-1), device(dz=2)]
    partners = [sibling, right, left, up, down, far_y] + z_next

    def split(a, h):
        return [a.at[0], a.at[1], a.at[2], h]

    w, snd, g = split(w_a, w_h), split(snd_a, snd_h), split(g_a, g_h)
    yr, x1, x2 = split(yr_a, yr_h), split(x1_a, x1_h), split(x2_a, x2_h)
    zr, yh, fin, sw = split(zr_a, zr_h), split(yh_a, yh_h), split(fin_a, fin_h), split(sw_a, sw_h)

    sent = []

    def send(src, dst, to):
        i = len(sent)
        copy = pltpu.make_async_remote_copy(
            src_ref=src, dst_ref=dst, send_sem=ssem.at[i], recv_sem=rsem.at[i],
            device_id=to, device_id_type=MESH,
        )
        copy.start()
        sent.append(copy)
        return copy

    local = []

    def fetch(src, dst):
        copy = pltpu.make_async_copy(src, dst, lsem.at[len(local)])
        copy.start()
        local.append(copy)
        return copy

    def hidden_cols(core):
        return pl.ds(pl.multiple_of(core * 384, 128), 512)

    got_master = fetch(master, mst)
    got_tok = fetch(tokens, tok.at[pl.ds(0, TOK)])
    got_hid = fetch(hidden.at[:, hidden_cols(c)], hid.at[pl.ds(0, TOK)])

    barrier = pltpu.get_barrier_semaphore()
    for p in partners:
        pl.semaphore_signal(barrier, inc=1, device_id=p, device_id_type=MESH)
    pl.semaphore_wait(barrier, len(partners))

    my_rows = pl.ds(pl.multiple_of(c * HALF, HALF), HALF)
    other_rows = pl.ds(pl.multiple_of((1 - c) * HALF, HALF), HALF)

    def cols(core, k, part):
        return pl.ds(pl.multiple_of(part * FFW + (core * 4 + k) * 128, 128), 128)

    low = lax.broadcasted_iota(jnp.int32, (HALF, 128), 1) < 64
    got_master.wait()
    swapped = []
    for k in range(NCHUNK):
        if k < 3:
            for part in range(2):
                there = pl.ds(part * 128, 128)
                snd[k][:, there] = mst[:, cols(1 - c, k, part)].astype(bf16)
                w[k][mine, my_rows, there] = mst[:, cols(c, k, part)].astype(bf16)
        else:
            gate, upw = mst[:, 384:512], pltpu.roll(mst[:, FFW + 384 : FFW + 512], 64, 1)
            own_first = jnp.logical_xor(low, jnp.broadcast_to(c == 1, low.shape))
            w[k][mine, my_rows, :] = jnp.where(own_first, gate, upw).astype(bf16)
            snd[k][...] = jnp.where(own_first, upw, gate).astype(bf16)
        swapped.append(send(snd[k], w[k].at[mine, my_rows], sibling))
    tok_in = send(tokens, tok.at[pl.ds(TOK, TOK)], sibling)
    hid_in = send(hidden.at[:, hidden_cols(1 - c)], hid.at[pl.ds(TOK, TOK)], sibling)

    A, B, ALL = pl.ds(0, 256), pl.ds(256, 256), pl.ds(0, 512)
    gat = [{} for _ in range(NCHUNK)]

    def unit_x(dx):
        return y_lo * 4 + (x + dx + 4) % 4

    def relay(k, unit, rows, to):
        part = w[k].at[unit, rows]
        return send(part, part, to)

    def to_y(k, name, unit):
        gat[k][name] = (relay(k, unit, A, up), relay(k, unit, B, down))

    def ag_start(k):
        swapped[k].wait_recv()
        gat[k]["right"] = relay(k, mine, ALL, right)
        gat[k]["left"] = relay(k, mine, ALL, left)
        to_y(k, "y0", mine)

    def ag_relay(k):
        gat[k]["right"].wait_recv()
        gat[k]["p"] = relay(k, unit_x(-1), A, right)
        gat[k]["left"].wait_recv()
        gat[k]["q"] = relay(k, unit_x(1), B, left)
        to_y(k, "y1", unit_x(-1))
        to_y(k, "y2", unit_x(1))

    def ag_relay2(k):
        gat[k]["p"].wait_recv()
        gat[k]["q"].wait_recv()
        to_y(k, "y3", unit_x(2))

    def ag_done(k):
        for name in ("y0", "y1", "y2", "y3"):
            for copy in gat[k][name]:
                copy.wait_recv()

    def transpose(half):
        @pl.loop(0, 8)
        def _(i):
            cut = pl.ds(pl.multiple_of(i * 512, 512), 512)
            tok_t[cut, pl.ds(half * TOK, TOK)] = tok[pl.ds(half * TOK, TOK), cut].T

    def start_col(k):
        return sum(WIDTHS[:k])

    def forward(k):
        n = WIDTHS[k]

        @pl.loop(0, 4)
        def _(i):
            rows = pl.ds(pl.multiple_of(i * 256, 256), 256)
            gu = jnp.dot(tok[rows, :], w[k][...].reshape(D, n), preferred_element_type=f32) * MULT
            if k < 3:
                h = hid[rows, pl.ds(pl.multiple_of((c + k) * 128, 128), 128)].astype(f32)
                gate, upw = gu[:, :128], gu[:, 128:]
            else:
                h = hid[rows, pl.ds(pl.multiple_of((1 - c) * 384, 128), 128)].astype(f32)
                gate, upw = gu, pltpu.roll(gu, 64, 1)
            s = jax.nn.sigmoid(gate)
            d_gate = h * upw * s * (1.0 + gate * (1.0 - s))
            d_up = h * gate * s
            if k < 3:
                branch[rows, pl.ds(start_col(k), 128)] = d_gate.astype(bf16)
                branch[rows, pl.ds(start_col(k) + 128, 128)] = d_up.astype(bf16)
            else:
                first = lax.broadcasted_iota(jnp.int32, gu.shape, 1) < 64
                own = jnp.logical_xor(first, jnp.broadcast_to(c == 1, gu.shape))
                mixed = jnp.where(own, d_gate, pltpu.roll(d_up, 64, 1))
                branch[rows, pl.ds(start_col(k), 128)] = mixed.astype(bf16)

    def gradient(k, base):
        n = WIDTHS[k]

        @pl.loop(0, 8)
        def _(i):
            unit = base + i // 2
            part = pl.multiple_of((i % 2) * 256, 256)
            rows = pl.ds(pl.multiple_of(unit * UNIT + part, 256), 256)
            got = jnp.dot(tok_t[rows, :], branch[:, pl.ds(start_col(k), n)], preferred_element_type=f32)
            g[k][unit, pl.ds(part, 256), :] = (got * MULT).astype(bf16)

    red = [{} for _ in range(NCHUNK)]

    def rs_y(k):
        theirs = pl.ds((1 - y_lo) * 4, 4)
        red[k]["yA"] = send(g[k].at[theirs, A], yr[k].at[:, A], up)
        red[k]["yB"] = send(g[k].at[theirs, B], yr[k].at[:, B], down)

    def rs_x1(k):
        red[k]["yA"].wait_recv()
        red[k]["yB"].wait_recv()
        for dx in (2, -1, 1, 0):
            xx = (x + dx + 4) % 4
            g[k][y_lo * 4 + xx] = add(g[k][y_lo * 4 + xx], yr[k][xx]).astype(bf16)
            if dx == 2:
                red[k]["p"] = send(g[k].at[unit_x(2), A], x1[k].at[A], right)
                red[k]["q"] = send(g[k].at[unit_x(2), B], x1[k].at[B], left)

    def rs_x2(k):
        red[k]["p"].wait_recv()
        unit = unit_x(1)
        g[k][unit, A, :] = add(g[k][unit, A, :], x1[k][A, :]).astype(bf16)
        red[k]["right"] = send(g[k].at[unit], x2[k].at[0], right)
        red[k]["q"].wait_recv()
        unit = unit_x(-1)
        g[k][unit, B, :] = add(g[k][unit, B, :], x1[k][B, :]).astype(bf16)
        red[k]["left"] = send(g[k].at[unit], x2[k].at[1], left)

    def quarter(dz):
        return pl.ds(pl.multiple_of(((z + dz + 4) % 4) * 128, 128), 128)

    def rs_z(k):
        red[k]["right"].wait_recv()
        red[k]["left"].wait_recv()
        g[k][mine] = add(g[k][mine], x2[k][0], x2[k][1]).astype(bf16)
        for j, dz in enumerate((1, -1, 2)):
            red[k][f"z{j}"] = send(g[k].at[mine, quarter(dz)], zr[k].at[j], z_next[j])

    def rs_yh(k):
        for j in range(3):
            red[k][f"z{j}"].wait_recv()
        total = add(g[k][mine, quarter(0), :], zr[k][0], zr[k][1], zr[k][2])
        yh[k][0] = total.astype(bf16)
        red[k]["yh"] = send(yh[k].at[0], yh[k].at[1], far_y)

    def rs_back(k):
        red[k]["yh"].wait_recv()
        fin[k][quarter(0), :] = add(yh[k][0], yh[k][1]).astype(bf16)
        for j in range(3):
            part = fin[k].at[quarter(0)]
            red[k][f"f{j}"] = send(part, part, z_next[j])

    def rs_swap(k):
        for j in range(3):
            red[k][f"f{j}"].wait_recv()
        red[k]["swap"] = send(fin[k].at[other_rows], sw[k], sibling)

    def rs_done(k):
        red[k]["swap"].wait_recv()
        if k < 3:
            for part in range(2):
                here = pl.ds(part * 128, 128)
                g_out[:, cols(c, k, part)] = fin[k][my_rows, here]
                g_out[:, cols(1 - c, k, part)] = sw[k][:, here]
        else:
            own = jnp.logical_xor(low, jnp.broadcast_to(c == 1, low.shape))
            mixed, theirs = fin[k][my_rows, :].astype(f32), sw[k][...].astype(f32)
            g_out[:, 384:512] = jnp.where(own, mixed, theirs).astype(bf16)
            g_out[:, FFW + 384 : FFW + 512] = pltpu.roll(jnp.where(own, theirs, mixed), 64, 1).astype(bf16)

    ig = {}

    def ig_dot(rows, unit):
        total = None
        for k in range(NCHUNK):
            part = lax.dot_general(
                branch[rows, pl.ds(start_col(k), WIDTHS[k])], w[k][unit],
                (((1,), (1,)), ((), ())), preferred_element_type=f32,
            )
            total = part if total is None else total + part
        return total * MULT

    def group_cols(j):
        return pl.ds(j * 2048, 2048)

    def ig_theirs(j):
        @pl.loop(0, 8)
        def _(i):
            unit = j * 4 + i // 2
            row = pl.multiple_of((i % 2) * 256, 256)
            cut = pl.ds(pl.multiple_of(unit * 512, 512), 512)
            tok[pl.ds(row, 256), cut] = ig_dot(pl.ds(TOK + row, 256), unit).astype(bf16)

        ig[j] = send(tok.at[pl.ds(0, TOK), group_cols(j)], ig_in.at[:, group_cols(j)], sibling)

    def ig_mine(j):
        ig[j].wait_recv()

        @pl.loop(0, 8)
        def _(i):
            unit = j * 4 + i // 2
            row = pl.multiple_of((i % 2) * 256, 256)
            cut = pl.ds(pl.multiple_of(unit * 512, 512), 512)
            value = ig_dot(pl.ds(row, 256), unit) + ig_in[pl.ds(row, 256), cut].astype(f32)
            tok[pl.ds(TOK + row, 256), cut] = value.astype(bf16)

        ig[j, "out"] = fetch(tok.at[pl.ds(TOK, TOK), group_cols(j)], ig_out.at[:, group_cols(j)])

    ag_start(0)
    ag_start(1)
    got_tok.wait()
    transpose(0)
    ag_relay(0)
    ag_relay2(0)
    ag_start(2)
    tok_in.wait_recv()
    transpose(1)
    got_hid.wait()
    hid_in.wait_recv()
    ag_done(0)
    ag_relay(1)
    forward(0)
    gradient(0, (1 - y_lo) * 4)
    rs_y(0)
    ag_relay2(1)
    ag_start(3)
    gradient(0, y_lo * 4)
    ag_relay(2)
    rs_x1(0)
    ag_done(1)
    forward(1)
    rs_x2(0)
    ag_relay2(2)
    ag_relay(3)
    gradient(1, (1 - y_lo) * 4)
    rs_y(1)
    rs_z(0)
    gradient(1, y_lo * 4)
    ag_relay2(3)
    rs_x1(1)
    ag_done(2)
    rs_yh(0)
    forward(2)
    rs_x2(1)
    rs_back(0)
    gradient(2, (1 - y_lo) * 4)
    rs_y(2)
    rs_z(1)
    gradient(2, y_lo * 4)
    ag_done(3)
    forward(3)
    rs_x1(2)
    gradient(3, (1 - y_lo) * 4)
    rs_y(3)
    rs_yh(1)
    rs_x2(2)
    gradient(3, y_lo * 4)
    rs_swap(0)
    ig_theirs(0)
    rs_x1(3)
    rs_back(1)
    rs_z(2)
    ig_theirs(1)
    rs_x2(3)
    rs_done(0)
    rs_yh(2)
    ig_mine(0)
    rs_z(3)
    rs_swap(1)
    rs_back(2)
    ig_mine(1)
    rs_yh(3)
    rs_done(1)
    rs_swap(2)
    rs_back(3)
    rs_done(2)
    rs_swap(3)
    rs_done(3)
    ig[0, "out"].wait()
    ig[1, "out"].wait()
    for copy in sent:
        copy.wait_send()


def fused(tokens, hidden, master):
    def pair(*shape):
        return [pltpu.VMEM((3, *shape, 256), bf16), pltpu.VMEM((*shape, 128), bf16)]

    anywhere = pl.BlockSpec(memory_space=pl.ANY)
    vmem = pl.BlockSpec(memory_space=pltpu.VMEM)
    return pl.pallas_call(
        kernel,
        out_shape=[jax.ShapeDtypeStruct((TOK, D), bf16), jax.ShapeDtypeStruct((HALF, 2 * FFW), bf16)],
        in_specs=[anywhere] * 3,
        out_specs=[anywhere, vmem],
        scratch_shapes=[
            pltpu.VMEM((2 * TOK, D), bf16),
            pltpu.VMEM((D, 2 * TOK), bf16),
            pltpu.VMEM((2 * TOK, 512), bf16),
            pltpu.VMEM((HALF, 2 * FFW), f32),
            pltpu.VMEM((2 * TOK, FFW), bf16),
            pltpu.VMEM((TOK, D), bf16),
            *pair(8, UNIT),
            *pair(HALF),
            *pair(8, UNIT),
            *pair(4, UNIT),
            *pair(UNIT),
            *pair(2, UNIT),
            *pair(3, 128),
            *pair(2, 128),
            *pair(UNIT),
            *pair(HALF),
            pltpu.SemaphoreType.DMA((8,)),
            pltpu.SemaphoreType.DMA((N_SEM,)),
            pltpu.SemaphoreType.DMA((N_SEM,)),
        ],
        compiler_params=pltpu.CompilerParams(
            collective_id=0, has_side_effects=True, vmem_limit_bytes=60 * 2**20
        ),
        cost_estimate=pl.CostEstimate(flops=22_500_000_000, bytes_accessed=20_000_000, transcendentals=1_000_000),
    )(tokens, hidden, master)


def body(tokens, hidden_grad, master, moment_first, moment_second):
    input_grad, grad = fused(tokens, hidden_grad, master)
    master_next, first_next, second_next = adamw(master, moment_first, moment_second, grad.astype(f32))
    return (input_grad, master_next, first_next, second_next)


def solution(mesh):
    return jax.shard_map(
        body,
        mesh=mesh,
        in_specs=(
            P(("rep", "shard"), None),
            P(("rep", "shard"), None),
            P("shard", None),
            P("shard", None),
            P("shard", None),
        ),
        out_specs=(P(("rep", "shard"), None), P("shard", None), P("shard", None), P("shard", None)),
        check_vma=False,
    )
```

time: 319 us -> 144 us (0.45); the launches traced: 315 us -> 143 us
  waiting for transfers between devices: 239 us -> 0 us
  Pallas kernels: 0 us -> 135 us
  matrix products: 35.9 us -> 0 us
  local copies, waits for them, and re-layouts: 16.3 us -> 2.03 us
  between operations: 13.8 us -> 0.68 us
  other arithmetic: 9.1 us -> 5.31 us
    pallas_call x0 -> x1, Pallas kernels: none -> 135 us  [fused(): pl.pallas_call(kernel, out_shape=[jax.ShapeDtypeStruct((TOK, D), bf16), j...]
    all_gather x1 -> x0, waiting for transfers between devices: 85.8 us -> none  [body(): gathered = lax.all_gather(weights_local, 'shard', axis=0, tiled=True)]
    reduce_scatter x1 -> x0, waiting for transfers between devices: 79 us -> none  [body(): lax.psum_scatter((contract_rows(tokens, branch_grad) * multiplier).astype...]
    psum x1 -> x0, waiting for transfers between devices: 74.6 us -> none  [body(): total = lax.psum(grad, 'rep').astype(jnp.float32)]
    dot_general x3 -> x0, matrix products: 35.9 us -> none  [the longest x1 12.7 us: contract_cols(): lax.dot_general(left, right, (((1,), (1,)), ((), ())), preferred_element_...]
    unnamed x20 -> x7, local copies, waits for them, and re-layouts: 16.3 us -> 2.03 us
  transfers between devices with their start and end apart: 3 -> 0, of which waited for: 3 -> 0; matrix products, arithmetic and copies ran while one was open for 6% -> 0% of each run, Pallas kernels for 0% -> 0%
where the time goes in v1:
time: 144 us; the launch traced here: 143 us
  Pallas kernels  135 us (94%)
  other arithmetic  5.31 us (4%)
  local copies, waits for them, and re-layouts  2.03 us (1%)
    pallas_call x1, Pallas kernels, fused(): pl.pallas_call(kernel, out_shape=[jax.ShapeDtypeStruct((TOK, D), bf16), j...  135 us
    sub x1, other arithmetic, adamw(): return (master - 0.01 * update, first_next, second_next)  5.31 us

profile of v1, /device:TPU:1, one launch (start us, length us, event | category | flops | bytes accessed | tf_op | source)
XLA Modules:
  0.0 143.5 jit_solution(16171930023548875369)
XLA Ops:
  0.6 0.0 copy-start.1
  0.6 0.0 copy-start.2
  0.7 135.5 %shard_map.84 = (bf16[512,4096]{1,0:T(8,128)(2,1)}, bf16[256,1792]{1,0:T(8,128)(2,1)}) custom-call(bf16[512,4096]{1,0:T(8,128)(2,1)} %tokens.1, bf16[512,896]{1,0:T(8,128)(2,1)} %hidden.1, f32[256,1792]{1,0:T(8,128)} %master.1), custom_call_target="tpu_custom_call" | custom-call | flops 22499999744 | bytes 20000000 | tf_op jit(solution)/shard_map/pallas_call | solution.py:396
  136.1 0.0 copy-done.1
  136.2 0.0 copy-done.2
  136.2 0.0 copy-start
  136.2 5.3 %multiply_subtract_fusion = (f32[256,1792]{1,0:T(8,128)}, f32[256,1792]{1,0:T(8,128)}, f32[256,1792]{1,0:T(8,128)}) fusion(f32[256,1792]{1,0:T(8,128)S(1)} %copy-done.1, bf16[256,1792]{1,0:T(8,128)(2,1)} %get-tuple-element.7, f32[256,1792]{1,0:T(8,128)S(1)} %copy-done.2, f32[256,1792]{1,0:T(8,128)} %param.9), kind=kLoop, calls=%fused_computation.4 | loop fusion | flops 7340032 | bytes 11927552 | tf_op jit(solution)/shard_map/sub | solution.py:28
  141.5 0.0 copy-done
  141.5 2.0 %copy.10 = bf16[512,4096]{1,0:T(8,128)(2,1)} copy(bf16[512,4096]{1,0:T(8,128)(2,1)S(1)} %copy-done) | data formatting | bytes 8388608
Async XLA Ops:
  0.6 135.5 %copy-start.1 = (f32[256,1792]{1,0:T(8,128)S(1)}, f32[256,1792]{1,0:T(8,128)}, u32[]{:S(2)}) copy-start(f32[256,1792]{1,0:T(8,128)} %master.1) | copy-start | bytes 5505028
  0.6 135.5 %copy-start.2 = (f32[256,1792]{1,0:T(8,128)S(1)}, f32[256,1792]{1,0:T(8,128)}, u32[]{:S(2)}) copy-start(f32[256,1792]{1,0:T(8,128)} %param.8) | copy-start | bytes 5505028
  136.2 5.3 %copy-start = (bf16[512,4096]{1,0:T(8,128)(2,1)S(1)}, bf16[512,4096]{1,0:T(8,128)(2,1)}, u32[]{:S(2)}) copy-start(bf16[512,4096]{1,0:T(8,128)(2,1)} %get-tuple-element.15) | copy-start | bytes 12582916

commit v2 on v0

v2 whole, which is shorter than its diff:
```python
import jax
import jax.numpy as jnp
from jax import lax
from jax.experimental import pallas as pl
from jax.experimental.pallas import tpu as pltpu
from jax.sharding import PartitionSpec as P

MESH = pl.DeviceIdType.MESH
bias_first = 0.999973438601
bias_second = 0.99407947078
bf16, f32 = jnp.bfloat16, jnp.float32

D, FFW, TOK = 4096, 896, 512
UNIT = 512
HALF = 256
MULT = 1.0 / 64.0
CHUNKS = ((0, 0), (1, 0), (2, 0), (3, 1))
GATHER = ((('xf', 0, 512),), (('yf', 0, 256), ('zq', 256, 256)), (('xf', 0, 128), ('zq', 128, 384)), (('xf', 0, 128), ('zq', 128, 384)))
REDUCE = ((('yf', 0, 256), ('xf', 256, 256)), (('yf', 0, 384), ('xf', 384, 128)), (('yf', 0, 384), ('xf', 384, 128)), (('yf', 0, 512),))
PLAN = (
    ('start', 0, 0), ('transpose', 0), ('transpose', 1), ('relay1', 0, 0), ('start', 1, 0),
    ('start', 1, 1), ('start', 2, 0), ('start', 2, 1), ('start', 3, 0), ('start', 3, 1),
    ('relay2', 0, 0), ('relay1', 1, 1), ('relay1', 1, 0), ('relay2', 1, 0), ('relay1', 2, 0),
    ('relay1', 2, 1), ('relay1', 3, 0), ('relay1', 3, 1), ('relay2', 1, 1), ('forward', 0),
    ('relay3', 1, 0), ('relay2', 2, 0), ('grad', 0, 0), ('relay3', 1, 1), ('pass1', 1, 1),
    ('relay2', 2, 1), ('relay2', 3, 0), ('relay2', 3, 1), ('grad', 0, 1), ('grad', 0, 2),
    ('grad', 0, 3), ('x1a', 0, 0), ('pass2', 1, 1), ('relay3', 2, 1), ('rs_x2', 0, 1),
    ('relay3', 3, 1), ('pass1', 2, 1), ('pass1', 3, 1), ('x1b', 0, 0), ('rs_x2', 0, 0),
    ('forward', 1), ('grad', 1, 0), ('x3', 0, 1), ('pass2', 2, 1), ('grad', 1, 1),
    ('pass2', 3, 1), ('grad', 1, 2), ('grad', 1, 3), ('x1a', 1, 0), ('rs_x2', 1, 1),
    ('forward', 2), ('rs_z', 0), ('grad', 2, 0), ('grad', 2, 1), ('x1b', 1, 0),
    ('rs_x2', 1, 0), ('x3', 1, 1), ('grad', 2, 2), ('grad', 2, 3), ('rs_yh', 0),
    ('x1a', 2, 0), ('rs_x2', 2, 1), ('forward', 3), ('grad', 3, 0), ('grad', 3, 1),
    ('grad', 3, 2), ('grad', 3, 3), ('ig_theirs', 0), ('rs_z', 1), ('x1b', 2, 0),
    ('rs_x2', 2, 0), ('x3', 2, 1), ('back', 0), ('x1a', 3, 0), ('ig_theirs', 1),
    ('ig_theirs', 2), ('x1b', 3, 0), ('rs_yh', 1), ('ig_theirs', 3), ('rs_z', 2),
    ('swap', 0), ('done', 0), ('rs_x2', 3, 0), ('ig_mine', 0), ('back', 1),
    ('ig_mine', 1), ('rs_z', 3), ('ig_mine', 2), ('rs_yh', 2), ('ig_mine', 3),
    ('swap', 1), ('done', 1), ('rs_yh', 3), ('back', 2), ('back', 3),
    ('swap', 2), ('done', 2), ('swap', 3), ('done', 3),
)

WIDTHS = tuple(128 if half else 256 for _, half in CHUNKS)
NCHUNK = len(CHUNKS)
N_SEM = 400


def adamw(master, moment_first, moment_second, grad):
    first_next = 0.9 * moment_first + 0.1 * grad
    second_next = 0.95 * moment_second + 0.05 * grad * grad
    corrected_one = first_next / bias_first
    corrected_two = second_next / bias_second
    update = corrected_one / (jnp.sqrt(corrected_two) + 1e-08) + 0.1 * master
    return (master - 0.01 * update, first_next, second_next)


def add(*values):
    total = values[0].astype(f32)
    for v in values[1:]:
        total = total + v.astype(f32)
    return total


def start_col(k):
    return sum(WIDTHS[:k])


def buffers(n, k):
    shapes = [(8, UNIT, n), (HALF, n), (8, UNIT, n), (4, UNIT, n), (2, UNIT, n), (2, 2, UNIT, n)]
    shapes += [(3, 128, n), (2, 128, n), (UNIT, n), (HALF, n)]
    return [pltpu.VMEM(shape, bf16) for shape in shapes]


N_BUF = 10


def kernel(tokens, hidden, master, ig_out, g_out, tok, tok_t, hid, mst, branch, ig_in, *rest):
    per_chunk = [rest[i * N_BUF : (i + 1) * N_BUF] for i in range(NCHUNK)]
    w, snd, g, yr, x1, x2, zr, yh, fin, sw = zip(*per_chunk)
    lsem, ssem, rsem = rest[NCHUNK * N_BUF :]

    rep, shard = lax.axis_index("rep"), lax.axis_index("shard")
    z, y_hi = rep // 2, rep % 2
    y_lo, x, c = shard // 8, (shard // 2) % 4, shard % 2
    y = y_hi * 2 + y_lo
    mine = y_lo * 4 + x
    across = (1 - y_lo) * 4 + x

    def device(dx=0, dy=0, dz=0, dc=0):
        xx, yy, zz, cc = (x + dx + 4) % 4, (y + dy + 4) % 4, (z + dz + 4) % 4, (c + dc) % 2
        return (zz * 2 + yy // 2, ((yy % 2) * 4 + xx) * 2 + cc)

    sibling = device(dc=1)
    right, left = device(dx=1), device(dx=-1)
    up, down = device(dy=1), device(dy=-1)
    far_y = device(dy=2)
    z_next = [device(dz=1), device(dz=-1), device(dz=2)]
    partners = [sibling, right, left, up, down, far_y] + z_next

    sent = []

    def send(src, dst, to):
        i = len(sent)
        copy = pltpu.make_async_remote_copy(
            src_ref=src, dst_ref=dst, send_sem=ssem.at[i], recv_sem=rsem.at[i],
            device_id=to, device_id_type=MESH,
        )
        copy.start()
        sent.append(copy)
        return copy

    local = []

    def fetch(src, dst):
        copy = pltpu.make_async_copy(src, dst, lsem.at[len(local)])
        copy.start()
        local.append(copy)
        return copy

    def hidden_cols(core):
        return pl.ds(pl.multiple_of(core * 384, 128), 512)

    got_master = fetch(master, mst)
    got_tok = fetch(tokens, tok.at[pl.ds(0, TOK)])
    got_hid = fetch(hidden.at[:, hidden_cols(c)], hid.at[pl.ds(0, TOK)])

    barrier = pltpu.get_barrier_semaphore()
    for p in partners:
        pl.semaphore_signal(barrier, inc=1, device_id=p, device_id_type=MESH)
    pl.semaphore_wait(barrier, len(partners))

    my_rows = pl.ds(pl.multiple_of(c * HALF, HALF), HALF)
    other_rows = pl.ds(pl.multiple_of((1 - c) * HALF, HALF), HALF)

    def block_of(core, k):
        b = CHUNKS[k][0]
        return 3 if b == 3 else core * 4 + b

    def cols(core, k, part):
        return pl.ds(pl.multiple_of(part * FFW + block_of(core, k) * 128, 128), 128)

    def side(core, k):
        return core if CHUNKS[k][0] == 3 else CHUNKS[k][1] - 1

    def gate_lanes(core, k, shape):
        low = lax.broadcasted_iota(jnp.int32, shape, 1) < 64
        return jnp.logical_xor(low, jnp.broadcast_to(side(core, k) == 1, shape))

    def chunk_of(core, k):
        gate, upw = mst[:, cols(core, k, 0)], mst[:, cols(core, k, 1)]
        if CHUNKS[k][1]:
            return [jnp.where(gate_lanes(core, k, gate.shape), gate, pltpu.roll(upw, 64, 1)).astype(bf16)]
        return [gate.astype(bf16), upw.astype(bf16)]

    got_master.wait()
    swapped = []
    for k in range(NCHUNK):
        for i, (ours, others) in enumerate(zip(chunk_of(c, k), chunk_of(1 - c, k))):
            w[k][mine, my_rows, pl.ds(i * 128, 128)] = ours
            snd[k][:, pl.ds(i * 128, 128)] = others
        swapped.append(send(snd[k], w[k].at[mine, my_rows], sibling))
    tok_in = send(tokens, tok.at[pl.ds(TOK, TOK)], sibling)
    hid_in = send(hidden.at[:, hidden_cols(1 - c)], hid.at[pl.ds(TOK, TOK)], sibling)

    def unit_x(dx):
        return y_lo * 4 + (x + dx + 4) % 4

    gat = {}
    theirs4 = pl.ds((1 - y_lo) * 4, 4)

    def relay(k, unit, rows, to):
        part = w[k].at[unit, rows]
        return send(part, part, to)

    class Rows:
        def __init__(self, k, m):
            self.mode, base, size = GATHER[k][m]
            self.base, self.size = base, size
            if self.mode == "zq":
                size = size // 4
                base = base + z * size
            step = size // 2
            align = 16
            self.all = pl.ds(pl.multiple_of(base, align), size)
            self.a = pl.ds(pl.multiple_of(base, align), step)
            self.b = pl.ds(pl.multiple_of(base + step, align), step)

        def along_z(self, dz, second):
            step = self.size // 8
            first = self.base + ((z + dz + 4) % 4) * (self.size // 4) + second * step
            return pl.ds(pl.multiple_of(first, 16), step)

    part_of = {(k, m): Rows(k, m) for k in range(NCHUNK) for m in range(len(GATHER[k]))}

    def to_y(k, m, name, unit):
        r = part_of[k, m]
        gat[k, m, name] = (relay(k, unit, r.a, up), relay(k, unit, r.b, down))

    def to_z(k, m, name, unit):
        r = part_of[k, m]
        gat[k, m, name] = (relay(k, unit, r.all, z_next[0]), relay(k, unit, r.all, z_next[1]))

    def on_z(k, m, name, unit):
        r = part_of[k, m]
        gat[k, m, name][0].wait_recv()
        first = relay(k, unit, r.along_z(-1, 0), z_next[0])
        gat[k, m, name][1].wait_recv()
        gat[k, m, name + "f"] = (first, relay(k, unit, r.along_z(1, 1), z_next[1]))

    def landed(k, m, *names):
        for name in names:
            for copy in gat[k, m, name]:
                copy.wait_recv()

    def both_x(k, m, name, unit):
        r = part_of[k, m]
        gat[k, m, name] = (relay(k, unit, r.all, right), relay(k, unit, r.all, left))

    def on_x(k, m, name, row):
        r = part_of[k, m]
        gat[k, m, name][0].wait_recv()
        first = relay(k, row * 4 + (x + 3) % 4, r.a, right)
        gat[k, m, name][1].wait_recv()
        gat[k, m, name + "f"] = (first, relay(k, row * 4 + (x + 1) % 4, r.b, left))

    def start(k, m):
        if m == 0:
            swapped[k].wait_recv()
        if part_of[k, m].mode == "yf":
            to_y(k, m, "y", mine)
            both_x(k, m, "x", mine)
        else:
            both_x(k, m, "x", mine)
            to_y(k, m, "y0", mine)

    def relay1(k, m):
        mode = part_of[k, m].mode
        if mode == "yf":
            landed(k, m, "y")
            both_x(k, m, "o", across)
            return
        on_x(k, m, "x", y_lo)
        to_y(k, m, "y1", unit_x(-1))
        to_y(k, m, "y2", unit_x(1))
        if mode == "zq":
            to_z(k, m, "z1", unit_x(-1))
            to_z(k, m, "z2", unit_x(1))

    def relay2(k, m):
        mode = part_of[k, m].mode
        if mode == "yf":
            on_x(k, m, "x", y_lo)
            return
        landed(k, m, "xf")
        to_y(k, m, "y3", unit_x(2))
        if mode == "zq":
            to_z(k, m, "z3", unit_x(2))

    def relay3(k, m):
        if part_of[k, m].mode == "yf":
            on_x(k, m, "o", 1 - y_lo)
            return
        landed(k, m, "y0", "y1", "y2", "y3")
        to_z(k, m, "z4", theirs4)

    def pass1(k, m):
        on_z(k, m, "z1", unit_x(-1))
        on_z(k, m, "z2", unit_x(1))
        on_z(k, m, "z3", unit_x(2))

    def pass2(k, m):
        on_z(k, m, "z4", theirs4)

    def gathered(k):
        for m in range(len(GATHER[k])):
            mode = part_of[k, m].mode
            if mode == "yf":
                landed(k, m, "xf", "of")
            elif mode == "xf":
                landed(k, m, "y0", "y1", "y2", "y3")
            else:
                landed(k, m, "z1f", "z2f", "z3f", "z4f")

    def transpose(half):
        (got_tok.wait, tok_in.wait_recv)[half]()

        @pl.loop(0, 8)
        def _(i):
            cut = pl.ds(pl.multiple_of(i * 512, 512), 512)
            tok_t[cut, pl.ds(half * TOK, TOK)] = tok[pl.ds(half * TOK, TOK), cut].T

        if half == 1:
            got_hid.wait()
            hid_in.wait_recv()

    def forward(k):
        gathered(k)
        n, here = WIDTHS[k], start_col(k)
        block = CHUNKS[k][0]
        at = (1 - c) * 384 if block == 3 else (c + block) * 128

        @pl.loop(0, 4)
        def _(i):
            rows = pl.ds(pl.multiple_of(i * 256, 256), 256)
            gu = jnp.dot(tok[rows, :], w[k][...].reshape(D, n), preferred_element_type=f32) * MULT
            h = hid[rows, pl.ds(pl.multiple_of(at, 128), 128)].astype(f32)
            half = CHUNKS[k][1]
            gate, upw = (gu, pltpu.roll(gu, 64, 1)) if half else (gu[:, :128], gu[:, 128:])
            s = jax.nn.sigmoid(gate)
            d_gate = h * upw * s * (1.0 + gate * (1.0 - s))
            d_up = h * gate * s
            if half:
                mixed = jnp.where(gate_lanes(c, k, gu.shape), d_gate, pltpu.roll(d_up, 64, 1))
                branch[rows, pl.ds(here, 128)] = mixed.astype(bf16)
            else:
                branch[rows, pl.ds(here, 128)] = d_gate.astype(bf16)
                branch[rows, pl.ds(here + 128, 128)] = d_up.astype(bf16)

    red = {}

    def in_turn(j):
        return (x + 2 + j) % 4

    def halves(base, size):
        return pl.ds(base, size // 2), pl.ds(base + size // 2, size // 2)

    def grad(k, j):
        n = WIDTHS[k]

        @pl.loop(0, 4)
        def _(i):
            unit = ((i // 2 + 1 - y_lo) % 2) * 4 + in_turn(j)
            part = pl.multiple_of((i % 2) * 256, 256)
            rows = pl.ds(pl.multiple_of(unit * UNIT + part, 256), 256)
            got = jnp.dot(tok_t[rows, :], branch[:, pl.ds(start_col(k), n)], preferred_element_type=f32)
            g[k][unit, pl.ds(part, 256), :] = (got * MULT).astype(bf16)

        for m, (mode, base, size) in enumerate(REDUCE[k]):
            a, b = halves(base, size)
            if mode == "yf":
                unit = (1 - y_lo) * 4 + in_turn(j)
                red[k, m, "y", j] = (
                    send(g[k].at[unit, a], yr[k].at[in_turn(j), a], up),
                    send(g[k].at[unit, b], yr[k].at[in_turn(j), b], down),
                )
            elif j == 0:
                red[k, m, "x1"] = [
                    (send(g[k].at[u * 4 + in_turn(0), a], x1[k].at[u, a], right),
                     send(g[k].at[u * 4 + in_turn(0), b], x1[k].at[u, b], left))
                    for u in range(2)
                ]

    def plus(k, unit, rows, *others):
        g[k][unit, rows, :] = add(g[k][unit, rows, :], *others).astype(bf16)

    def take_y(k, m, j):
        _, base, size = REDUCE[k][m]
        for copy in red[k, m, "y", j]:
            copy.wait_recv()
        rows = pl.ds(base, size)
        plus(k, y_lo * 4 + in_turn(j), rows, yr[k][in_turn(j), rows, :])

    def x1a(k, m):
        _, base, size = REDUCE[k][m]
        a, b = halves(base, size)
        take_y(k, m, 0)
        red[k, m, "p"] = send(g[k].at[unit_x(2), a], x1[k].at[0, a], right)
        red[k, m, "q"] = send(g[k].at[unit_x(2), b], x1[k].at[0, b], left)

    def x1b(k, m):
        for j in range(1, 4):
            take_y(k, m, j)

    def rs_x2(k, m):
        mode, base, size = REDUCE[k][m]
        rows, (a, b) = pl.ds(base, size), halves(base, size)
        if mode == "yf":
            red[k, m, "p"].wait_recv()
            plus(k, unit_x(1), a, x1[k][0, a, :])
            red[k, m, "r"] = [send(g[k].at[unit_x(1), rows], x2[k].at[0, 0, rows], right)]
            red[k, m, "q"].wait_recv()
            plus(k, unit_x(-1), b, x1[k][0, b, :])
            red[k, m, "l"] = [send(g[k].at[unit_x(-1), rows], x2[k].at[1, 0, rows], left)]
            return
        red[k, m, "r"], red[k, m, "l"] = [], []
        for u in range(2):
            p, q = red[k, m, "x1"][u]
            here = u * 4 + (x + 1) % 4
            p.wait_recv()
            plus(k, here, a, x1[k][u, a, :])
            red[k, m, "r"].append(send(g[k].at[here, rows], x2[k].at[0, u, rows], right))
            here = u * 4 + (x + 3) % 4
            q.wait_recv()
            plus(k, here, b, x1[k][u, b, :])
            red[k, m, "l"].append(send(g[k].at[here, rows], x2[k].at[1, u, rows], left))

    def x3(k, m):
        _, base, size = REDUCE[k][m]
        rows, (a, b) = pl.ds(base, size), halves(base, size)
        for copy in red[k, m, "r"] + red[k, m, "l"]:
            copy.wait_recv()
        for u in range(2):
            plus(k, u * 4 + x, rows, x2[k][0, u, rows, :], x2[k][1, u, rows, :])
        red[k, m, "ya"] = (
            send(g[k].at[across, a], yr[k].at[0, a], up),
            send(g[k].at[across, b], yr[k].at[0, b], down),
        )

    def quarter(dz):
        return pl.ds(pl.multiple_of(((z + dz + 4) % 4) * 128, 128), 128)

    def rs_z(k):
        for m, (mode, base, size) in enumerate(REDUCE[k]):
            rows = pl.ds(base, size)
            if mode == "yf":
                for copy in red[k, m, "r"] + red[k, m, "l"]:
                    copy.wait_recv()
                plus(k, mine, rows, x2[k][0, 0, rows, :], x2[k][1, 0, rows, :])
            else:
                for copy in red[k, m, "ya"]:
                    copy.wait_recv()
                plus(k, mine, rows, yr[k][0, rows, :])
        red[k, "z"] = [send(g[k].at[mine, quarter(dz)], zr[k].at[j], z_next[j]) for j, dz in enumerate((1, -1, 2))]

    def rs_yh(k):
        for copy in red[k, "z"]:
            copy.wait_recv()
        total = add(g[k][mine, quarter(0), :], zr[k][0], zr[k][1], zr[k][2])
        yh[k][0] = total.astype(bf16)
        red[k, "yh"] = send(yh[k].at[0], yh[k].at[1], far_y)

    def back(k):
        red[k, "yh"].wait_recv()
        fin[k][quarter(0), :] = add(yh[k][0], yh[k][1]).astype(bf16)
        part = fin[k].at[quarter(0)]
        red[k, "back"] = [send(part, part, z_next[j]) for j in range(3)]

    def swap(k):
        for copy in red[k, "back"]:
            copy.wait_recv()
        red[k, "swap"] = send(fin[k].at[other_rows], sw[k], sibling)

    def done(k):
        red[k, "swap"].wait_recv()
        own, theirs = fin[k][my_rows, :], sw[k][...]
        block, half = CHUNKS[k]
        if not half:
            for core, value in ((c, own), (1 - c, theirs)):
                g_out[:, cols(core, k, 0)] = value[:, :128]
                g_out[:, cols(core, k, 1)] = value[:, 128:]
            return
        gates = gate_lanes(c, k, own.shape)
        if block == 3:
            g_out[:, cols(c, k, 0)] = jnp.where(gates, own, theirs)
            g_out[:, cols(c, k, 1)] = pltpu.roll(jnp.where(gates, theirs, own).astype(f32), 64, 1).astype(bf16)
            return
        for core, value in ((c, own), (1 - c, theirs)):
            for part, lanes in ((0, value), (1, pltpu.roll(value.astype(f32), 64, 1).astype(bf16))):
                if half == 2:
                    lanes = jnp.where(gates, lanes, g_out[:, cols(core, k, part)])
                g_out[:, cols(core, k, part)] = lanes

    ig = {}

    def ig_dot(rows, unit):
        total = None
        for k in range(NCHUNK):
            part = lax.dot_general(
                branch[rows, pl.ds(start_col(k), WIDTHS[k])], w[k][unit],
                (((1,), (1,)), ((), ())), preferred_element_type=f32,
            )
            total = part if total is None else total + part
        return total * MULT

    def group_cols(j):
        return pl.ds(j * 1024, 1024)

    def ig_theirs(j):
        @pl.loop(0, 4)
        def _(i):
            unit = j * 2 + i // 2
            row = pl.multiple_of((i % 2) * 256, 256)
            cut = pl.ds(pl.multiple_of(unit * 512, 512), 512)
            tok[pl.ds(row, 256), cut] = ig_dot(pl.ds(TOK + row, 256), unit).astype(bf16)

        ig[j] = send(tok.at[pl.ds(0, TOK), group_cols(j)], ig_in.at[:, group_cols(j)], sibling)

    def ig_mine(j):
        ig[j].wait_recv()

        @pl.loop(0, 4)
        def _(i):
            unit = j * 2 + i // 2
            row = pl.multiple_of((i % 2) * 256, 256)
            cut = pl.ds(pl.multiple_of(unit * 512, 512), 512)
            value = ig_dot(pl.ds(row, 256), unit) + ig_in[pl.ds(row, 256), cut].astype(f32)
            tok[pl.ds(TOK + row, 256), cut] = value.astype(bf16)

        ig[j, "out"] = fetch(tok.at[pl.ds(TOK, TOK), group_cols(j)], ig_out.at[:, group_cols(j)])

    steps = dict(
        start=start, relay1=relay1, relay2=relay2, relay3=relay3, pass1=pass1, pass2=pass2, transpose=transpose,
        forward=forward, grad=grad, x1a=x1a, x1b=x1b, rs_x2=rs_x2, x3=x3, rs_z=rs_z, rs_yh=rs_yh, back=back,
        swap=swap, done=done, ig_theirs=ig_theirs, ig_mine=ig_mine,
    )
    for name, *which in PLAN:
        steps[name](*which)
    for j in range(4):
        ig[j, "out"].wait()
    for copy in sent:
        copy.wait_send()


def fused(tokens, hidden, master):
    anywhere = pl.BlockSpec(memory_space=pl.ANY)
    vmem = pl.BlockSpec(memory_space=pltpu.VMEM)
    return pl.pallas_call(
        kernel,
        out_shape=[jax.ShapeDtypeStruct((TOK, D), bf16), jax.ShapeDtypeStruct((HALF, 2 * FFW), bf16)],
        in_specs=[anywhere] * 3,
        out_specs=[anywhere, vmem],
        scratch_shapes=[
            pltpu.VMEM((2 * TOK, D), bf16),
            pltpu.VMEM((D, 2 * TOK), bf16),
            pltpu.VMEM((2 * TOK, 512), bf16),
            pltpu.VMEM((HALF, 2 * FFW), f32),
            pltpu.VMEM((2 * TOK, FFW), bf16),
            pltpu.VMEM((TOK, D), bf16),
            *(ref for k in range(NCHUNK) for ref in buffers(WIDTHS[k], k)),
            pltpu.SemaphoreType.DMA((8,)),
            pltpu.SemaphoreType.DMA((N_SEM,)),
            pltpu.SemaphoreType.DMA((N_SEM,)),
        ],
        compiler_params=pltpu.CompilerParams(
            collective_id=0, has_side_effects=True, vmem_limit_bytes=63 * 2**20
        ),
        cost_estimate=pl.CostEstimate(flops=22_500_000_000, bytes_accessed=20_000_000, transcendentals=1_000_000),
    )(tokens, hidden, master)


def body(tokens, hidden_grad, master, moment_first, moment_second):
    input_grad, grad = fused(tokens, hidden_grad, master)
    master_next, first_next, second_next = adamw(master, moment_first, moment_second, grad.astype(f32))
    return (input_grad, master_next, first_next, second_next)


def solution(mesh):
    return jax.shard_map(
        body,
        mesh=mesh,
        in_specs=(
            P(("rep", "shard"), None),
            P(("rep", "shard"), None),
            P("shard", None),
            P("shard", None),
            P("shard", None),
        ),
        out_specs=(P(("rep", "shard"), None), P("shard", None), P("shard", None), P("shard", None)),
        check_vma=False,
    )
```

time: 319 us -> 121 us (0.38); the launches traced: 315 us -> 121 us
  waiting for transfers between devices: 239 us -> 0 us
  Pallas kernels: 0 us -> 112 us
  matrix products: 35.9 us -> 0 us
  local copies, waits for them, and re-layouts: 16.3 us -> 2.02 us
  between operations: 13.8 us -> 0.65 us
    pallas_call x0 -> x1, Pallas kernels: none -> 112 us  [fused(): pl.pallas_call(kernel, out_shape=[jax.ShapeDtypeStruct((TOK, D), bf16), j...]
    all_gather x1 -> x0, waiting for transfers between devices: 85.8 us -> none  [body(): gathered = lax.all_gather(weights_local, 'shard', axis=0, tiled=True)]
    reduce_scatter x1 -> x0, waiting for transfers between devices: 79 us -> none  [body(): lax.psum_scatter((contract_rows(tokens, branch_grad) * multiplier).astype...]
    psum x1 -> x0, waiting for transfers between devices: 74.6 us -> none  [body(): total = lax.psum(grad, 'rep').astype(jnp.float32)]
    dot_general x3 -> x0, matrix products: 35.9 us -> none  [the longest x1 12.7 us: contract_cols(): lax.dot_general(left, right, (((1,), (1,)), ((), ())), preferred_element_...]
    unnamed x20 -> x3, local copies, waits for them, and re-layouts: 16.3 us -> 2.02 us
  transfers between devices with their start and end apart: 3 -> 0, of which waited for: 3 -> 0; matrix products, arithmetic and copies ran while one was open for 6% -> 0% of each run, Pallas kernels for 0% -> 0%
where the time goes in v2:
time: 121 us
  Pallas kernels  112 us (93%)
  other arithmetic  6.41 us (5%)
  local copies, waits for them, and re-layouts  2.02 us (2%)
    pallas_call x1, Pallas kernels, fused(): pl.pallas_call(kernel, out_shape=[jax.ShapeDtypeStruct((TOK, D), bf16), j...  112 us
    sub x1, other arithmetic, adamw(): return (master - 0.01 * update, first_next, second_next)  6.41 us

profile of v2, /device:TPU:1, one launch (start us, length us, event | category | flops | bytes accessed | tf_op | source)
XLA Modules:
  0.0 121.3 jit_solution(218955733490961256)
XLA Ops:
  0.6 112.2 %shard_map.84 = (bf16[512,4096]{1,0:T(8,128)(2,1)}, bf16[256,1792]{1,0:T(8,128)(2,1)}) custom-call(bf16[512,4096]{1,0:T(8,128)(2,1)} %tokens.1, bf16[512,896]{1,0:T(8,128)(2,1)} %hidden.1, f32[256,1792]{1,0:T(8,128)} %master.1), custom_call_target="tpu_custom_call" | custom-call | flops 22499999744 | bytes 20000000 | tf_op jit(solution)/shard_map/pallas_call | solution.py:517
  112.8 0.0 copy-start
  112.9 6.4 %multiply_subtract_fusion = (f32[256,1792]{1,0:T(8,128)}, f32[256,1792]{1,0:T(8,128)}, f32[256,1792]{1,0:T(8,128)}) fusion(f32[256,1792]{1,0:T(8,128)} %master.1, bf16[256,1792]{1,0:T(8,128)(2,1)} %get-tuple-element.7, f32[256,1792]{1,0:T(8,128)} %param.8, f32[256,1792]{1,0:T(8,128)} %param.9), kind=kLoop, calls=%fused_computation.4 | loop fusion | flops 7340032 | bytes 11927552 | tf_op jit(solution)/shard_map/sub | solution.py:54
  119.3 0.0 copy-done
  119.3 2.0 %copy.10 = bf16[512,4096]{1,0:T(8,128)(2,1)} copy(bf16[512,4096]{1,0:T(8,128)(2,1)S(1)} %copy-done) | data formatting | bytes 8388608
Async XLA Ops:
  112.8 6.4 %copy-start = (bf16[512,4096]{1,0:T(8,128)(2,1)S(1)}, bf16[512,4096]{1,0:T(8,128)(2,1)}, u32[]{:S(2)}) copy-start(bf16[512,4096]{1,0:T(8,128)(2,1)} %get-tuple-element.15) | copy-start | bytes 12582916

commit v3 on v2

--- a/solution.py
+++ b/solution.py
@@ -1,3 +1,5 @@
+import math
+
 import jax
 import jax.numpy as jnp
 from jax import lax
@@ -42,7 +44,7 @@
 
 WIDTHS = tuple(128 if half else 256 for _, half in CHUNKS)
 NCHUNK = len(CHUNKS)
-N_SEM = 400
+N_IN, N_OUT = 90, 7
 
 
 def adamw(master, moment_first, moment_second, grad):
@@ -97,17 +99,46 @@
     z_next = [device(dz=1), device(dz=-1), device(dz=2)]
     partners = [sibling, right, left, up, down, far_y] + z_next
 
-    sent = []
-
-    def send(src, dst, to):
-        i = len(sent)
-        copy = pltpu.make_async_remote_copy(
-            src_ref=src, dst_ref=dst, send_sem=ssem.at[i], recv_sem=rsem.at[i],
+    def cut_of(size):
+        tiles, left_over = divmod(size, 16 * 128 * 2)
+        fits = [wide for wide in range(1, 9) if tiles % wide == 0 and tiles // wide <= D // 16]
+        return (tiles // fits[-1] * 16, fits[-1] * 128) if fits and not left_over else None
+
+    def some_bytes(size):
+        rows, columns = cut_of(size)
+        return tok_t.at[pl.ds(0, rows), pl.ds(0, columns)]
+
+    outgoing, inboxes = [], []
+
+    def awaiting(size, out, into):
+        ref = some_bytes(size)
+        return pltpu.make_async_remote_copy(
+            src_ref=ref, dst_ref=ref, send_sem=ssem.at[out], recv_sem=rsem.at[into],
+            device_id=sibling, device_id_type=MESH,
+        )
+
+    class Inbox:
+        def __init__(self):
+            self.index, self.size, self.waited = len(inboxes), 0, False
+            inboxes.append(self)
+
+        def wait_recv(self):
+            assert self.size and not self.waited
+            self.waited = True
+            awaiting(self.size, 0, self.index).wait_recv()
+
+    def send(src, dst, to, into=None):
+        into = Inbox() if into is None else into
+        size = 2 * math.prod(src.shape)
+        if not outgoing or (outgoing[-1] > 3 * 2**20 and cut_of(outgoing[-1])):
+            outgoing.append(0)
+        outgoing[-1] += size
+        into.size += size
+        pltpu.make_async_remote_copy(
+            src_ref=src, dst_ref=dst, send_sem=ssem.at[len(outgoing) - 1], recv_sem=rsem.at[into.index],
             device_id=to, device_id_type=MESH,
-        )
-        copy.start()
-        sent.append(copy)
-        return copy
+        ).start()
+        return into
 
     local = []
 
@@ -168,9 +199,14 @@
     gat = {}
     theirs4 = pl.ds((1 - y_lo) * 4, 4)
 
-    def relay(k, unit, rows, to):
+    def relay(k, unit, rows, to, into):
         part = w[k].at[unit, rows]
-        return send(part, part, to)
+        send(part, part, to, into)
+
+    def inbox(*key):
+        if key not in gat:
+            gat[key] = Inbox()
+        return gat[key]
 
     class Rows:
         def __init__(self, k, m):
@@ -194,34 +230,32 @@
 
     def to_y(k, m, name, unit):
         r = part_of[k, m]
-        gat[k, m, name] = (relay(k, unit, r.a, up), relay(k, unit, r.b, down))
+        relay(k, unit, r.a, up, inbox(k, m, name))
+        relay(k, unit, r.b, down, inbox(k, m, name))
 
     def to_z(k, m, name, unit):
         r = part_of[k, m]
-        gat[k, m, name] = (relay(k, unit, r.all, z_next[0]), relay(k, unit, r.all, z_next[1]))
-
-    def on_z(k, m, name, unit):
+        for there in z_next[:2]:
+            relay(k, unit, r.all, there, inbox(k, m, name))
+
+    def on_z(k, m, unit):
         r = part_of[k, m]
-        gat[k, m, name][0].wait_recv()
-        first = relay(k, unit, r.along_z(-1, 0), z_next[0])
-        gat[k, m, name][1].wait_recv()
-        gat[k, m, name + "f"] = (first, relay(k, unit, r.along_z(1, 1), z_next[1]))
-
-    def landed(k, m, *names):
-        for name in names:
-            for copy in gat[k, m, name]:
-                copy.wait_recv()
+        relay(k, unit, r.along_z(-1, 0), z_next[0], inbox(k, m, "zf"))
+        relay(k, unit, r.along_z(1, 1), z_next[1], inbox(k, m, "zf"))
+
+    def landed(*key):
+        gat[key].wait_recv()
 
     def both_x(k, m, name, unit):
         r = part_of[k, m]
-        gat[k, m, name] = (relay(k, unit, r.all, right), relay(k, unit, r.all, left))
+        for there in (right, left):
+            relay(k, unit, r.all, there, inbox(k, m, name))
 
     def on_x(k, m, name, row):
         r = part_of[k, m]
-        gat[k, m, name][0].wait_recv()
-        first = relay(k, row * 4 + (x + 3) % 4, r.a, right)
-        gat[k, m, name][1].wait_recv()
-        gat[k, m, name + "f"] = (first, relay(k, row * 4 + (x + 1) % 4, r.b, left))
+        landed(k, m, name)
+        relay(k, row * 4 + (x + 3) % 4, r.a, right, inbox(k, m, "xf"))
+        relay(k, row * 4 + (x + 1) % 4, r.b, left, inbox(k, m, "xf"))
 
     def start(k, m):
         if m == 0:
@@ -231,7 +265,7 @@
             both_x(k, m, "x", mine)
         else:
             both_x(k, m, "x", mine)
-            to_y(k, m, "y0", mine)
+            to_y(k, m, "y", mine)
 
     def relay1(k, m):
         mode = part_of[k, m].mode
@@ -240,11 +274,10 @@
             both_x(k, m, "o", across)
             return
         on_x(k, m, "x", y_lo)
-        to_y(k, m, "y1", unit_x(-1))
-        to_y(k, m, "y2", unit_x(1))
-        if mode == "zq":
-            to_z(k, m, "z1", unit_x(-1))
-            to_z(k, m, "z2", unit_x(1))
+        for dx in (-1, 1):
+            to_y(k, m, "y", unit_x(dx))
+            if mode == "zq":
+                to_z(k, m, "z", unit_x(dx))
 
     def relay2(k, m):
         mode = part_of[k, m].mode
@@ -252,34 +285,29 @@
             on_x(k, m, "x", y_lo)
             return
         landed(k, m, "xf")
-        to_y(k, m, "y3", unit_x(2))
+        to_y(k, m, "y", unit_x(2))
         if mode == "zq":
-            to_z(k, m, "z3", unit_x(2))
+            to_z(k, m, "z", unit_x(2))
 
     def relay3(k, m):
         if part_of[k, m].mode == "yf":
             on_x(k, m, "o", 1 - y_lo)
             return
-        landed(k, m, "y0", "y1", "y2", "y3")
+        landed(k, m, "y")
         to_z(k, m, "z4", theirs4)
 
     def pass1(k, m):
-        on_z(k, m, "z1", unit_x(-1))
-        on_z(k, m, "z2", unit_x(1))
-        on_z(k, m, "z3", unit_x(2))
+        landed(k, m, "z")
+        for dx in (-1, 1, 2):
+            on_z(k, m, unit_x(dx))
 
     def pass2(k, m):
-        on_z(k, m, "z4", theirs4)
+        landed(k, m, "z4")
+        on_z(k, m, theirs4)
 
     def gathered(k):
         for m in range(len(GATHER[k])):
-            mode = part_of[k, m].mode
-            if mode == "yf":
-                landed(k, m, "xf", "of")
-            elif mode == "xf":
-                landed(k, m, "y0", "y1", "y2", "y3")
-            else:
-                landed(k, m, "z1f", "z2f", "z3f", "z4f")
+            landed(k, m, {"yf": "xf", "xf": "y", "zq": "zf"}[part_of[k, m].mode])
 
     def transpose(half):
         (got_tok.wait, tok_in.wait_recv)[half]()
@@ -299,9 +327,9 @@
         block = CHUNKS[k][0]
         at = (1 - c) * 384 if block == 3 else (c + block) * 128
 
-        @pl.loop(0, 4)
+        @pl.loop(0, 2)
         def _(i):
-            rows = pl.ds(pl.multiple_of(i * 256, 256), 256)
+            rows = pl.ds(pl.multiple_of(i * 512, 512), 512)
             gu = jnp.dot(tok[rows, :], w[k][...].reshape(D, n), preferred_element_type=f32) * MULT
             h = hid[rows, pl.ds(pl.multiple_of(at, 128), 128)].astype(f32)
             half = CHUNKS[k][1]
@@ -327,36 +355,32 @@
     def grad(k, j):
         n = WIDTHS[k]
 
-        @pl.loop(0, 4)
+        @pl.loop(0, 2)
         def _(i):
-            unit = ((i // 2 + 1 - y_lo) % 2) * 4 + in_turn(j)
-            part = pl.multiple_of((i % 2) * 256, 256)
-            rows = pl.ds(pl.multiple_of(unit * UNIT + part, 256), 256)
+            unit = ((i + 1 - y_lo) % 2) * 4 + in_turn(j)
+            rows = pl.ds(pl.multiple_of(unit * UNIT, UNIT), UNIT)
             got = jnp.dot(tok_t[rows, :], branch[:, pl.ds(start_col(k), n)], preferred_element_type=f32)
-            g[k][unit, pl.ds(part, 256), :] = (got * MULT).astype(bf16)
+            g[k][unit] = (got * MULT).astype(bf16)
 
         for m, (mode, base, size) in enumerate(REDUCE[k]):
             a, b = halves(base, size)
             if mode == "yf":
-                unit = (1 - y_lo) * 4 + in_turn(j)
-                red[k, m, "y", j] = (
-                    send(g[k].at[unit, a], yr[k].at[in_turn(j), a], up),
-                    send(g[k].at[unit, b], yr[k].at[in_turn(j), b], down),
-                )
+                unit, box = (1 - y_lo) * 4 + in_turn(j), Inbox()
+                send(g[k].at[unit, a], yr[k].at[in_turn(j), a], up, box)
+                send(g[k].at[unit, b], yr[k].at[in_turn(j), b], down, box)
+                red[k, m, "y", j] = box
             elif j == 0:
-                red[k, m, "x1"] = [
-                    (send(g[k].at[u * 4 + in_turn(0), a], x1[k].at[u, a], right),
-                     send(g[k].at[u * 4 + in_turn(0), b], x1[k].at[u, b], left))
-                    for u in range(2)
-                ]
+                red[k, m, "x1"] = box = Inbox()
+                for u in range(2):
+                    send(g[k].at[u * 4 + in_turn(0), a], x1[k].at[u, a], right, box)
+                    send(g[k].at[u * 4 + in_turn(0), b], x1[k].at[u, b], left, box)
 
     def plus(k, unit, rows, *others):
         g[k][unit, rows, :] = add(g[k][unit, rows, :], *others).astype(bf16)
 
     def take_y(k, m, j):
         _, base, size = REDUCE[k][m]
-        for copy in red[k, m, "y", j]:
-            copy.wait_recv()
+        red[k, m, "y", j].wait_recv()
         rows = pl.ds(base, size)
         plus(k, y_lo * 4 + in_turn(j), rows, yr[k][in_turn(j), rows, :])
 
@@ -364,8 +388,9 @@
         _, base, size = REDUCE[k][m]
         a, b = halves(base, size)
         take_y(k, m, 0)
-        red[k, m, "p"] = send(g[k].at[unit_x(2), a], x1[k].at[0, a], right)
-        red[k, m, "q"] = send(g[k].at[unit_x(2), b], x1[k].at[0, b], left)
+        red[k, m, "x1"] = box = Inbox()
+        send(g[k].at[unit_x(2), a], x1[k].at[0, a], right, box)
+        send(g[k].at[unit_x(2), b], x1[k].at[0, b], left, box)
 
     def x1b(k, m):
         for j in range(1, 4):
@@ -374,37 +399,25 @@
     def rs_x2(k, m):
         mode, base, size = REDUCE[k][m]
         rows, (a, b) = pl.ds(base, size), halves(base, size)
-        if mode == "yf":
-            red[k, m, "p"].wait_recv()
-            plus(k, unit_x(1), a, x1[k][0, a, :])
-            red[k, m, "r"] = [send(g[k].at[unit_x(1), rows], x2[k].at[0, 0, rows], right)]
-            red[k, m, "q"].wait_recv()
-            plus(k, unit_x(-1), b, x1[k][0, b, :])
-            red[k, m, "l"] = [send(g[k].at[unit_x(-1), rows], x2[k].at[1, 0, rows], left)]
-            return
-        red[k, m, "r"], red[k, m, "l"] = [], []
-        for u in range(2):
-            p, q = red[k, m, "x1"][u]
-            here = u * 4 + (x + 1) % 4
-            p.wait_recv()
+        red[k, m, "x1"].wait_recv()
+        red[k, m, "x2"] = box = Inbox()
+        for u, row in ((0, y_lo),) if mode == "yf" else ((0, 0), (1, 1)):
+            here = row * 4 + (x + 1) % 4
             plus(k, here, a, x1[k][u, a, :])
-            red[k, m, "r"].append(send(g[k].at[here, rows], x2[k].at[0, u, rows], right))
-            here = u * 4 + (x + 3) % 4
-            q.wait_recv()
+            send(g[k].at[here, rows], x2[k].at[0, u, rows], right, box)
+            here = row * 4 + (x + 3) % 4
             plus(k, here, b, x1[k][u, b, :])
-            red[k, m, "l"].append(send(g[k].at[here, rows], x2[k].at[1, u, rows], left))
+            send(g[k].at[here, rows], x2[k].at[1, u, rows], left, box)
 
     def x3(k, m):
         _, base, size = REDUCE[k][m]
         rows, (a, b) = pl.ds(base, size), halves(base, size)
-        for copy in red[k, m, "r"] + red[k, m, "l"]:
-            copy.wait_recv()
+        red[k, m, "x2"].wait_recv()
         for u in range(2):
             plus(k, u * 4 + x, rows, x2[k][0, u, rows, :], x2[k][1, u, rows, :])
-        red[k, m, "ya"] = (
-            send(g[k].at[across, a], yr[k].at[0, a], up),
-            send(g[k].at[across, b], yr[k].at[0, b], down),
-        )
+        red[k, m, "y"] = box = Inbox()
+        send(g[k].at[across, a], yr[k].at[0, a], up, box)
+        send(g[k].at[across, b], yr[k].at[0, b], down, box)
 
     def quarter(dz):
         return pl.ds(pl.multiple_of(((z + dz + 4) % 4) * 128, 128), 128)
@@ -413,18 +426,17 @@
         for m, (mode, base, size) in enumerate(REDUCE[k]):
             rows = pl.ds(base, size)
             if mode == "yf":
-                for copy in red[k, m, "r"] + red[k, m, "l"]:
-                    copy.wait_recv()
+                red[k, m, "x2"].wait_recv()
                 plus(k, mine, rows, x2[k][0, 0, rows, :], x2[k][1, 0, rows, :])
             else:
-                for copy in red[k, m, "ya"]:
-                    copy.wait_recv()
+                red[k, m, "y"].wait_recv()
                 plus(k, mine, rows, yr[k][0, rows, :])
-        red[k, "z"] = [send(g[k].at[mine, quarter(dz)], zr[k].at[j], z_next[j]) for j, dz in enumerate((1, -1, 2))]
+        red[k, "z"] = box = Inbox()
+        for j, dz in enumerate((1, -1, 2)):
+            send(g[k].at[mine, quarter(dz)], zr[k].at[j], z_next[j], box)
 
     def rs_yh(k):
-        for copy in red[k, "z"]:
-            copy.wait_recv()
+        red[k, "z"].wait_recv()
         total = add(g[k][mine, quarter(0), :], zr[k][0], zr[k][1], zr[k][2])
         yh[k][0] = total.astype(bf16)
         red[k, "yh"] = send(yh[k].at[0], yh[k].at[1], far_y)
@@ -433,11 +445,12 @@
         red[k, "yh"].wait_recv()
         fin[k][quarter(0), :] = add(yh[k][0], yh[k][1]).astype(bf16)
         part = fin[k].at[quarter(0)]
-        red[k, "back"] = [send(part, part, z_next[j]) for j in range(3)]
+        red[k, "back"] = box = Inbox()
+        for j in range(3):
+            send(part, part, z_next[j], box)
 
     def swap(k):
-        for copy in red[k, "back"]:
-            copy.wait_recv()
+        red[k, "back"].wait_recv()
         red[k, "swap"] = send(fin[k].at[other_rows], sw[k], sibling)
 
     def done(k):
@@ -476,25 +489,23 @@
         return pl.ds(j * 1024, 1024)
 
     def ig_theirs(j):
-        @pl.loop(0, 4)
+        @pl.loop(0, 2)
         def _(i):
-            unit = j * 2 + i // 2
-            row = pl.multiple_of((i % 2) * 256, 256)
+            unit = j * 2 + i
             cut = pl.ds(pl.multiple_of(unit * 512, 512), 512)
-            tok[pl.ds(row, 256), cut] = ig_dot(pl.ds(TOK + row, 256), unit).astype(bf16)
+            tok[pl.ds(0, TOK), cut] = ig_dot(pl.ds(TOK, TOK), unit).astype(bf16)
 
         ig[j] = send(tok.at[pl.ds(0, TOK), group_cols(j)], ig_in.at[:, group_cols(j)], sibling)
 
     def ig_mine(j):
         ig[j].wait_recv()
 
-        @pl.loop(0, 4)
+        @pl.loop(0, 2)
         def _(i):
-            unit = j * 2 + i // 2
-            row = pl.multiple_of((i % 2) * 256, 256)
+            unit = j * 2 + i
             cut = pl.ds(pl.multiple_of(unit * 512, 512), 512)
-            value = ig_dot(pl.ds(row, 256), unit) + ig_in[pl.ds(row, 256), cut].astype(f32)
-            tok[pl.ds(TOK + row, 256), cut] = value.astype(bf16)
+            value = ig_dot(pl.ds(0, TOK), unit) + ig_in[:, cut].astype(f32)
+            tok[pl.ds(TOK, TOK), cut] = value.astype(bf16)
 
         ig[j, "out"] = fetch(tok.at[pl.ds(TOK, TOK), group_cols(j)], ig_out.at[:, group_cols(j)])
 
@@ -507,8 +518,9 @@
         steps[name](*which)
     for j in range(4):
         ig[j, "out"].wait()
-    for copy in sent:
-        copy.wait_send()
+    assert all(box.waited for box in inboxes) and len(inboxes) <= N_IN and len(outgoing) <= N_OUT
+    for i, size in enumerate(outgoing):
+        awaiting(size, i, 0).wait_send()
 
 
 def fused(tokens, hidden, master):
@@ -528,8 +540,8 @@
             pltpu.VMEM((TOK, D), bf16),
             *(ref for k in range(NCHUNK) for ref in buffers(WIDTHS[k], k)),
             pltpu.SemaphoreType.DMA((8,)),
-            pltpu.SemaphoreType.DMA((N_SEM,)),
-            pltpu.SemaphoreType.DMA((N_SEM,)),
+            pltpu.SemaphoreType.DMA((N_OUT,)),
+            pltpu.SemaphoreType.DMA((N_IN,)),
         ],
         compiler_params=pltpu.CompilerParams(
             collective_id=0, has_side_effects=True, vmem_limit_bytes=63 * 2**20

time: 121 us -> 111 us (0.917)
  Pallas kernels: 112 us -> 102 us
    pallas_call x1, Pallas kernels: 112 us -> 102 us  [fused(): pl.pallas_call(kernel, out_shape=[jax.ShapeDtypeStruct((TOK, D), bf16), j...]
where the time goes in v3:
time: 111 us
  Pallas kernels  102 us (92%)
  other arithmetic  6.41 us (6%)
  local copies, waits for them, and re-layouts  2.02 us (2%)
    pallas_call x1, Pallas kernels, fused(): pl.pallas_call(kernel, out_shape=[jax.ShapeDtypeStruct((TOK, D), bf16), j...  102 us
    sub x1, other arithmetic, adamw(): return (master - 0.01 * update, first_next, second_next)  6.41 us

profile of v3, /device:TPU:1, one launch (start us, length us, event | category | flops | bytes accessed | tf_op | source)
XLA Modules:
  0.0 110.7 jit_solution(9740710024695355464)
XLA Ops:
  0.6 101.6 %shard_map.84 = (bf16[512,4096]{1,0:T(8,128)(2,1)}, bf16[256,1792]{1,0:T(8,128)(2,1)}) custom-call(bf16[512,4096]{1,0:T(8,128)(2,1)} %tokens.1, bf16[512,896]{1,0:T(8,128)(2,1)} %hidden.1, f32[256,1792]{1,0:T(8,128)} %master.1), custom_call_target="tpu_custom_call" | custom-call | flops 22499999744 | bytes 20000000 | tf_op jit(solution)/shard_map/pallas_call | solution.py:529
  102.2 0.0 copy-start
  102.2 6.4 %multiply_subtract_fusion = (f32[256,1792]{1,0:T(8,128)}, f32[256,1792]{1,0:T(8,128)}, f32[256,1792]{1,0:T(8,128)}) fusion(f32[256,1792]{1,0:T(8,128)} %master.1, bf16[256,1792]{1,0:T(8,128)(2,1)} %get-tuple-element.7, f32[256,1792]{1,0:T(8,128)} %param.8, f32[256,1792]{1,0:T(8,128)} %param.9), kind=kLoop, calls=%fused_computation.4 | loop fusion | flops 7340032 | bytes 11927552 | tf_op jit(solution)/shard_map/sub | solution.py:56
  108.7 0.0 copy-done
  108.7 2.0 %copy.10 = bf16[512,4096]{1,0:T(8,128)(2,1)} copy(bf16[512,4096]{1,0:T(8,128)(2,1)S(1)} %copy-done) | data formatting | bytes 8388608
Async XLA Ops:
  102.2 6.4 %copy-start = (bf16[512,4096]{1,0:T(8,128)(2,1)S(1)}, bf16[512,4096]{1,0:T(8,128)(2,1)}, u32[]{:S(2)}) copy-start(bf16[512,4096]{1,0:T(8,128)(2,1)} %get-tuple-element.15) | copy-start | bytes 12582916

commit v4 on v3

--- a/solution.py
+++ b/solution.py
@@ -16,35 +16,36 @@
 UNIT = 512
 HALF = 256
 MULT = 1.0 / 64.0
-CHUNKS = ((0, 0), (1, 0), (2, 0), (3, 1))
-GATHER = ((('xf', 0, 512),), (('yf', 0, 256), ('zq', 256, 256)), (('xf', 0, 128), ('zq', 128, 384)), (('xf', 0, 128), ('zq', 128, 384)))
-REDUCE = ((('yf', 0, 256), ('xf', 256, 256)), (('yf', 0, 384), ('xf', 384, 128)), (('yf', 0, 384), ('xf', 384, 128)), (('yf', 0, 512),))
+CHUNKS = ((3, 1), (0, 0), (1, 0), (2, 0))
+FAR = (False, False, False, True)
+GATHER = ((('zq', 0, 512),), (('xf', 0, 128), ('yf', 128, 128), ('zq', 256, 256)), (('xf', 0, 256), ('zq', 256, 256)), (('xf', 0, 256), ('zq', 256, 256)))
+REDUCE = ((('xf', 0, 512),), (('yf', 0, 384), ('xf', 384, 128)), (('yf', 0, 384), ('xf', 384, 128)), (('yf', 0, 384), ('xf', 384, 128)))
 PLAN = (
-    ('start', 0, 0), ('transpose', 0), ('transpose', 1), ('relay1', 0, 0), ('start', 1, 0),
-    ('start', 1, 1), ('start', 2, 0), ('start', 2, 1), ('start', 3, 0), ('start', 3, 1),
-    ('relay2', 0, 0), ('relay1', 1, 1), ('relay1', 1, 0), ('relay2', 1, 0), ('relay1', 2, 0),
-    ('relay1', 2, 1), ('relay1', 3, 0), ('relay1', 3, 1), ('relay2', 1, 1), ('forward', 0),
-    ('relay3', 1, 0), ('relay2', 2, 0), ('grad', 0, 0), ('relay3', 1, 1), ('pass1', 1, 1),
-    ('relay2', 2, 1), ('relay2', 3, 0), ('relay2', 3, 1), ('grad', 0, 1), ('grad', 0, 2),
-    ('grad', 0, 3), ('x1a', 0, 0), ('pass2', 1, 1), ('relay3', 2, 1), ('rs_x2', 0, 1),
-    ('relay3', 3, 1), ('pass1', 2, 1), ('pass1', 3, 1), ('x1b', 0, 0), ('rs_x2', 0, 0),
-    ('forward', 1), ('grad', 1, 0), ('x3', 0, 1), ('pass2', 2, 1), ('grad', 1, 1),
-    ('pass2', 3, 1), ('grad', 1, 2), ('grad', 1, 3), ('x1a', 1, 0), ('rs_x2', 1, 1),
-    ('forward', 2), ('rs_z', 0), ('grad', 2, 0), ('grad', 2, 1), ('x1b', 1, 0),
-    ('rs_x2', 1, 0), ('x3', 1, 1), ('grad', 2, 2), ('grad', 2, 3), ('rs_yh', 0),
-    ('x1a', 2, 0), ('rs_x2', 2, 1), ('forward', 3), ('grad', 3, 0), ('grad', 3, 1),
-    ('grad', 3, 2), ('grad', 3, 3), ('ig_theirs', 0), ('rs_z', 1), ('x1b', 2, 0),
-    ('rs_x2', 2, 0), ('x3', 2, 1), ('back', 0), ('x1a', 3, 0), ('ig_theirs', 1),
-    ('ig_theirs', 2), ('x1b', 3, 0), ('rs_yh', 1), ('ig_theirs', 3), ('rs_z', 2),
-    ('swap', 0), ('done', 0), ('rs_x2', 3, 0), ('ig_mine', 0), ('back', 1),
-    ('ig_mine', 1), ('rs_z', 3), ('ig_mine', 2), ('rs_yh', 2), ('ig_mine', 3),
-    ('swap', 1), ('done', 1), ('rs_yh', 3), ('back', 2), ('back', 3),
-    ('swap', 2), ('done', 2), ('swap', 3), ('done', 3),
+    ('start', 0, 0), ('start', 1, 0), ('start', 1, 1), ('start', 1, 2), ('transpose', 0),
+    ('relay1', 0, 0), ('relay1', 1, 1), ('relay1', 1, 0), ('transpose', 1), ('relay2', 0, 0),
+    ('relay2', 1, 1), ('relay1', 1, 2), ('start', 2, 0), ('relay3', 1, 1), ('start', 2, 1),
+    ('relay2', 1, 0), ('relay3', 0, 0), ('start', 3, 0), ('pass1', 0, 0), ('start', 3, 1),
+    ('relay2', 1, 2), ('relay1', 2, 0), ('pass2', 0, 0), ('relay1', 2, 1), ('relay3', 1, 2),
+    ('pass1', 1, 2), ('relay1', 3, 0), ('forward', 0), ('relay2', 2, 0), ('relay2', 2, 1),
+    ('relay1', 3, 1), ('grad', 0, 0), ('relay2', 3, 0), ('pass2', 1, 2), ('grad', 0, 1),
+    ('grad', 0, 2), ('relay2', 3, 1), ('grad', 0, 3), ('relay3', 2, 1), ('pass1', 2, 1),
+    ('rs_x2', 0, 0), ('forward', 1), ('relay3', 3, 1), ('pass1', 3, 1), ('pass2', 2, 1),
+    ('grad', 1, 0), ('grad', 1, 1), ('grad', 1, 2), ('grad', 1, 3), ('x3', 0, 0),
+    ('pass2', 3, 1), ('x1a', 1, 0), ('rs_x2', 1, 1), ('forward', 2), ('grad', 2, 0),
+    ('grad', 2, 1), ('x1b', 1, 0), ('rs_x2', 1, 0), ('x3', 1, 1), ('rs_z', 0),
+    ('grad', 2, 2), ('grad', 2, 3), ('x1a', 2, 0), ('rs_x2', 2, 1), ('forward', 3),
+    ('rs_yh', 0), ('rs_z', 1), ('grad', 3, 0), ('grad', 3, 1), ('grad', 3, 2),
+    ('x1b', 2, 0), ('back', 0), ('rs_x2', 2, 0), ('x3', 2, 1), ('grad', 3, 3),
+    ('rs_yh', 1), ('x1a', 3, 0), ('rs_x2', 3, 1), ('ig_theirs', 0), ('done', 0),
+    ('ig_theirs', 1), ('ig_theirs', 2), ('rs_z', 2), ('x1b', 3, 0), ('rs_x2', 3, 0),
+    ('ig_theirs', 3), ('back', 1), ('x3', 3, 1), ('ig_mine', 0), ('rs_yh', 2),
+    ('ig_mine', 1), ('rs_z', 3), ('ig_mine', 2), ('done', 1), ('back', 2),
+    ('ig_mine', 3), ('back', 3), ('done', 2), ('done', 3),
 )
 
 WIDTHS = tuple(128 if half else 256 for _, half in CHUNKS)
 NCHUNK = len(CHUNKS)
-N_IN, N_OUT = 90, 7
+N_IN, N_OUT = 88, 14
 
 
 def adamw(master, moment_first, moment_second, grad):
@@ -69,16 +70,16 @@
 
 def buffers(n, k):
     shapes = [(8, UNIT, n), (HALF, n), (8, UNIT, n), (4, UNIT, n), (2, UNIT, n), (2, 2, UNIT, n)]
-    shapes += [(3, 128, n), (2, 128, n), (UNIT, n), (HALF, n)]
+    shapes += [(7, 64, n) if FAR[k] else (3, 128, n), (3, 128, n), (2, HALF, n)]
     return [pltpu.VMEM(shape, bf16) for shape in shapes]
 
 
-N_BUF = 10
+N_BUF = 9
 
 
 def kernel(tokens, hidden, master, ig_out, g_out, tok, tok_t, hid, mst, branch, ig_in, *rest):
     per_chunk = [rest[i * N_BUF : (i + 1) * N_BUF] for i in range(NCHUNK)]
-    w, snd, g, yr, x1, x2, zr, yh, fin, sw = zip(*per_chunk)
+    w, snd, g, yr, x1, x2, zr, yh, fin = zip(*per_chunk)
     lsem, ssem, rsem = rest[NCHUNK * N_BUF :]
 
     rep, shard = lax.axis_index("rep"), lax.axis_index("shard")
@@ -97,7 +98,10 @@
     up, down = device(dy=1), device(dy=-1)
     far_y = device(dy=2)
     z_next = [device(dz=1), device(dz=-1), device(dz=2)]
-    partners = [sibling, right, left, up, down, far_y] + z_next
+    across_x = device(dx=2)
+    group = [(dz, dy) for dy in (2, 0) for dz in (1, -1, 2, 0)]
+    partners = [right, left, across_x, up, down] + [device(dz=dz, dy=dy) for dz, dy in group[:7]]
+    partners += [device(dz=dz, dy=dy, dc=1) for dz, dy in group]
 
     def cut_of(size):
         tiles, left_over = divmod(size, 16 * 128 * 2)
@@ -108,6 +112,7 @@
         rows, columns = cut_of(size)
         return tok_t.at[pl.ds(0, rows), pl.ds(0, columns)]
 
+    only_apart = []
     outgoing, inboxes = [], []
 
     def awaiting(size, out, into):
@@ -161,7 +166,6 @@
     pl.semaphore_wait(barrier, len(partners))
 
     my_rows = pl.ds(pl.multiple_of(c * HALF, HALF), HALF)
-    other_rows = pl.ds(pl.multiple_of((1 - c) * HALF, HALF), HALF)
 
     def block_of(core, k):
         b = CHUNKS[k][0]
@@ -260,6 +264,8 @@
     def start(k, m):
         if m == 0:
             swapped[k].wait_recv()
+        if part_of[k, m].mode == "xd":
+            relay(k, mine, part_of[k, m].all, across_x, inbox(k, m, "xf"))
         if part_of[k, m].mode == "yf":
             to_y(k, m, "y", mine)
             both_x(k, m, "x", mine)
@@ -273,7 +279,10 @@
             landed(k, m, "y")
             both_x(k, m, "o", across)
             return
-        on_x(k, m, "x", y_lo)
+        if mode == "xd":
+            landed(k, m, "x")
+        else:
+            on_x(k, m, "x", y_lo)
         for dx in (-1, 1):
             to_y(k, m, "y", unit_x(dx))
             if mode == "zq":
@@ -307,7 +316,7 @@
 
     def gathered(k):
         for m in range(len(GATHER[k])):
-            landed(k, m, {"yf": "xf", "xf": "y", "zq": "zf"}[part_of[k, m].mode])
+            landed(k, m, {"yf": "xf", "xf": "y", "xd": "y", "zq": "zf"}[part_of[k, m].mode])
 
     def transpose(half):
         (got_tok.wait, tok_in.wait_recv)[half]()
@@ -364,7 +373,7 @@
 
         for m, (mode, base, size) in enumerate(REDUCE[k]):
             a, b = halves(base, size)
-            if mode == "yf":
+            if mode in ("yf", "yd"):
                 unit, box = (1 - y_lo) * 4 + in_turn(j), Inbox()
                 send(g[k].at[unit, a], yr[k].at[in_turn(j), a], up, box)
                 send(g[k].at[unit, b], yr[k].at[in_turn(j), b], down, box)
@@ -385,20 +394,30 @@
         plus(k, y_lo * 4 + in_turn(j), rows, yr[k][in_turn(j), rows, :])
 
     def x1a(k, m):
-        _, base, size = REDUCE[k][m]
-        a, b = halves(base, size)
+        mode, base, size = REDUCE[k][m]
+        rows, (a, b) = pl.ds(base, size), halves(base, size)
         take_y(k, m, 0)
+        if mode == "yd":
+            red[k, m, "x2"] = send(g[k].at[unit_x(2), rows], x2[k].at[0, 1, rows], across_x)
+            return
         red[k, m, "x1"] = box = Inbox()
         send(g[k].at[unit_x(2), a], x1[k].at[0, a], right, box)
         send(g[k].at[unit_x(2), b], x1[k].at[0, b], left, box)
 
     def x1b(k, m):
-        for j in range(1, 4):
+        mode, base, size = REDUCE[k][m]
+        rows = pl.ds(base, size)
+        for j in (1, 3, 2):
             take_y(k, m, j)
+            if mode == "yd" and j != 2:
+                there, slot = ((left, 1), None, (right, 0))[j - 1]
+                send(g[k].at[y_lo * 4 + in_turn(j), rows], x2[k].at[slot, 0, rows], there, red[k, m, "x2"])
 
     def rs_x2(k, m):
         mode, base, size = REDUCE[k][m]
         rows, (a, b) = pl.ds(base, size), halves(base, size)
+        if mode == "yd":
+            return
         red[k, m, "x1"].wait_recv()
         red[k, m, "x2"] = box = Inbox()
         for u, row in ((0, y_lo),) if mode == "yf" else ((0, 0), (1, 1)):
@@ -422,40 +441,74 @@
     def quarter(dz):
         return pl.ds(pl.multiple_of(((z + dz + 4) % 4) * 128, 128), 128)
 
+    def share(dz, dy):
+        return pl.ds(pl.multiple_of((((z + dz + 4) % 4) * 2 + (y_hi + dy // 2) % 2) * 64, 64), 64)
+
     def rs_z(k):
         for m, (mode, base, size) in enumerate(REDUCE[k]):
             rows = pl.ds(base, size)
-            if mode == "yf":
-                red[k, m, "x2"].wait_recv()
-                plus(k, mine, rows, x2[k][0, 0, rows, :], x2[k][1, 0, rows, :])
-            else:
+            if mode == "xf":
                 red[k, m, "y"].wait_recv()
                 plus(k, mine, rows, yr[k][0, rows, :])
+                continue
+            red[k, m, "x2"].wait_recv()
+            third = [x2[k][0, 1, rows, :]] if mode == "yd" else []
+            plus(k, mine, rows, x2[k][0, 0, rows, :], x2[k][1, 0, rows, :], *third)
         red[k, "z"] = box = Inbox()
+        if FAR[k]:
+            for j, (dz, dy) in enumerate(group[:7]):
+                send(g[k].at[mine, share(dz, dy)], zr[k].at[j], device(dz=dz, dy=dy), box)
+            return
         for j, dz in enumerate((1, -1, 2)):
             send(g[k].at[mine, quarter(dz)], zr[k].at[j], z_next[j], box)
 
     def rs_yh(k):
+        if FAR[k]:
+            return
         red[k, "z"].wait_recv()
         total = add(g[k][mine, quarter(0), :], zr[k][0], zr[k][1], zr[k][2])
         yh[k][0] = total.astype(bf16)
         red[k, "yh"] = send(yh[k].at[0], yh[k].at[1], far_y)
 
     def back(k):
-        red[k, "yh"].wait_recv()
-        fin[k][quarter(0), :] = add(yh[k][0], yh[k][1]).astype(bf16)
-        part = fin[k].at[quarter(0)]
+        owner, rows = z // 2, 64 if FAR[k] else 128
+        if FAR[k]:
+            red[k, "z"].wait_recv()
+            total = add(g[k][mine, share(0, 0), :], *(zr[k][j] for j in range(7)))
+            first = (z % 2) * 128 + y_hi * 64
+        else:
+            red[k, "yh"].wait_recv()
+            total = add(yh[k][0], yh[k][1])
+            first = (z % 2) * 128
+        part = yh[k].at[2, pl.ds(0, rows)]
+        part[...] = total.astype(bf16)
+        there = fin[k].at[c, pl.ds(pl.multiple_of(first, 64), rows)]
         red[k, "back"] = box = Inbox()
-        for j in range(3):
-            send(part, part, z_next[j], box)
-
-    def swap(k):
+        for dz, dy in group[:7] if FAR[k] else group[4:7]:
+            zz, yy = (z + dz + 4) % 4, (y + dy) % 4
+            send(part, there, (zz * 2 + yy // 2, (y_lo * 4 + x) * 2 + owner), box)
+        size = 2 * rows * WIDTHS[k]
+        box.size += size
+        outgoing.append(size)
+        alone = len(outgoing) - 1
+        only_apart.append(alone)
+
+        @pl.when(c != owner)
+        def _():
+            pltpu.make_async_remote_copy(
+                src_ref=part, dst_ref=there, send_sem=ssem.at[alone], recv_sem=rsem.at[box.index],
+                device_id=sibling, device_id_type=MESH,
+            ).start()
+
+        @pl.when(c == owner)
+        def _():
+            pltpu.make_async_copy(part, there, rsem.at[box.index]).start()
+
+        outgoing.append(0)
+
+    def done(k):
         red[k, "back"].wait_recv()
-        red[k, "swap"] = send(fin[k].at[other_rows], sw[k], sibling)
-
-    def done(k):
-        red[k, "swap"].wait_recv()
-        own, theirs = fin[k][my_rows, :], sw[k][...]
+        own, theirs = fin[k][c], fin[k][1 - c]
         block, half = CHUNKS[k]
         if not half:
             for core, value in ((c, own), (1 - c, theirs)):
@@ -512,7 +565,7 @@
     steps = dict(
         start=start, relay1=relay1, relay2=relay2, relay3=relay3, pass1=pass1, pass2=pass2, transpose=transpose,
         forward=forward, grad=grad, x1a=x1a, x1b=x1b, rs_x2=rs_x2, x3=x3, rs_z=rs_z, rs_yh=rs_yh, back=back,
-        swap=swap, done=done, ig_theirs=ig_theirs, ig_mine=ig_mine,
+        done=done, ig_theirs=ig_theirs, ig_mine=ig_mine,
     )
     for name, *which in PLAN:
         steps[name](*which)
@@ -520,7 +573,14 @@
         ig[j, "out"].wait()
     assert all(box.waited for box in inboxes) and len(inboxes) <= N_IN and len(outgoing) <= N_OUT
     for i, size in enumerate(outgoing):
-        awaiting(size, i, 0).wait_send()
+        if i in only_apart:
+
+            @pl.when(c != z // 2)
+            def _():
+                awaiting(size, i, 0).wait_send()
+
+        elif size:
+            awaiting(size, i, 0).wait_send()
 
 
 def fused(tokens, hidden, master):

time: 111 us -> 104 us (0.937)
  Pallas kernels: 102 us -> 95 us
    pallas_call x1, Pallas kernels: 102 us -> 95 us  [fused(): pl.pallas_call(kernel, out_shape=[jax.ShapeDtypeStruct((TOK, D), bf16), j...]
where the time goes in v4:
time: 104 us
  Pallas kernels  95 us (91%)
  other arithmetic  6.41 us (6%)
  local copies, waits for them, and re-layouts  2.02 us (2%)
    pallas_call x1, Pallas kernels, fused(): pl.pallas_call(kernel, out_shape=[jax.ShapeDtypeStruct((TOK, D), bf16), j...  95 us
    sub x1, other arithmetic, adamw(): return (master - 0.01 * update, first_next, second_next)  6.41 us

profile of v4, /device:TPU:1, one launch (start us, length us, event | category | flops | bytes accessed | tf_op | source)
XLA Modules:
  0.0 104.1 jit_solution(248629932498435501)
XLA Ops:
  0.6 95.0 %shard_map.84 = (bf16[512,4096]{1,0:T(8,128)(2,1)}, bf16[256,1792]{1,0:T(8,128)(2,1)}) custom-call(bf16[512,4096]{1,0:T(8,128)(2,1)} %tokens.1, bf16[512,896]{1,0:T(8,128)(2,1)} %hidden.1, f32[256,1792]{1,0:T(8,128)} %master.1), custom_call_target="tpu_custom_call" | custom-call | flops 22499999744 | bytes 20000000 | tf_op jit(solution)/shard_map/pallas_call | solution.py:589
  95.6 0.0 copy-start
  95.6 6.4 %multiply_subtract_fusion = (f32[256,1792]{1,0:T(8,128)}, f32[256,1792]{1,0:T(8,128)}, f32[256,1792]{1,0:T(8,128)}) fusion(f32[256,1792]{1,0:T(8,128)} %master.1, bf16[256,1792]{1,0:T(8,128)(2,1)} %get-tuple-element.7, f32[256,1792]{1,0:T(8,128)} %param.8, f32[256,1792]{1,0:T(8,128)} %param.9), kind=kLoop, calls=%fused_computation.4 | loop fusion | flops 7340032 | bytes 11927552 | tf_op jit(solution)/shard_map/sub | solution.py:57
  102.0 0.0 copy-done
  102.0 2.0 %copy.10 = bf16[512,4096]{1,0:T(8,128)(2,1)} copy(bf16[512,4096]{1,0:T(8,128)(2,1)S(1)} %copy-done) | data formatting | bytes 8388608
Async XLA Ops:
  95.6 6.4 %copy-start = (bf16[512,4096]{1,0:T(8,128)(2,1)S(1)}, bf16[512,4096]{1,0:T(8,128)(2,1)}, u32[]{:S(2)}) copy-start(bf16[512,4096]{1,0:T(8,128)(2,1)} %get-tuple-element.15) | copy-start | bytes 12582916

commit v5 on v4

--- a/solution.py
+++ b/solution.py
@@ -18,34 +18,34 @@
 MULT = 1.0 / 64.0
 CHUNKS = ((3, 1), (0, 0), (1, 0), (2, 0))
 FAR = (False, False, False, True)
-GATHER = ((('zq', 0, 512),), (('xf', 0, 128), ('yf', 128, 128), ('zq', 256, 256)), (('xf', 0, 256), ('zq', 256, 256)), (('xf', 0, 256), ('zq', 256, 256)))
-REDUCE = ((('xf', 0, 512),), (('yf', 0, 384), ('xf', 384, 128)), (('yf', 0, 384), ('xf', 384, 128)), (('yf', 0, 384), ('xf', 384, 128)))
+GATHER = ((('zq', 0, 512),), (('xf', 0, 128), ('yf', 128, 128), ('zq', 256, 256)), (('xf', 0, 256), ('yf', 256, 256)), (('zq', 0, 512),))
+REDUCE = ((('yf', 0, 256), ('xf', 256, 256)), (('yf', 0, 384), ('xf', 384, 128)), (('yf', 0, 384), ('xf', 384, 128)), (('yf', 0, 384), ('xf', 384, 128)))
 PLAN = (
     ('start', 0, 0), ('start', 1, 0), ('start', 1, 1), ('start', 1, 2), ('transpose', 0),
     ('relay1', 0, 0), ('relay1', 1, 1), ('relay1', 1, 0), ('transpose', 1), ('relay2', 0, 0),
     ('relay2', 1, 1), ('relay1', 1, 2), ('start', 2, 0), ('relay3', 1, 1), ('start', 2, 1),
-    ('relay2', 1, 0), ('relay3', 0, 0), ('start', 3, 0), ('pass1', 0, 0), ('start', 3, 1),
-    ('relay2', 1, 2), ('relay1', 2, 0), ('pass2', 0, 0), ('relay1', 2, 1), ('relay3', 1, 2),
-    ('pass1', 1, 2), ('relay1', 3, 0), ('forward', 0), ('relay2', 2, 0), ('relay2', 2, 1),
-    ('relay1', 3, 1), ('grad', 0, 0), ('relay2', 3, 0), ('pass2', 1, 2), ('grad', 0, 1),
-    ('grad', 0, 2), ('relay2', 3, 1), ('grad', 0, 3), ('relay3', 2, 1), ('pass1', 2, 1),
-    ('rs_x2', 0, 0), ('forward', 1), ('relay3', 3, 1), ('pass1', 3, 1), ('pass2', 2, 1),
-    ('grad', 1, 0), ('grad', 1, 1), ('grad', 1, 2), ('grad', 1, 3), ('x3', 0, 0),
-    ('pass2', 3, 1), ('x1a', 1, 0), ('rs_x2', 1, 1), ('forward', 2), ('grad', 2, 0),
-    ('grad', 2, 1), ('x1b', 1, 0), ('rs_x2', 1, 0), ('x3', 1, 1), ('rs_z', 0),
-    ('grad', 2, 2), ('grad', 2, 3), ('x1a', 2, 0), ('rs_x2', 2, 1), ('forward', 3),
-    ('rs_yh', 0), ('rs_z', 1), ('grad', 3, 0), ('grad', 3, 1), ('grad', 3, 2),
-    ('x1b', 2, 0), ('back', 0), ('rs_x2', 2, 0), ('x3', 2, 1), ('grad', 3, 3),
-    ('rs_yh', 1), ('x1a', 3, 0), ('rs_x2', 3, 1), ('ig_theirs', 0), ('done', 0),
-    ('ig_theirs', 1), ('ig_theirs', 2), ('rs_z', 2), ('x1b', 3, 0), ('rs_x2', 3, 0),
-    ('ig_theirs', 3), ('back', 1), ('x3', 3, 1), ('ig_mine', 0), ('rs_yh', 2),
-    ('ig_mine', 1), ('rs_z', 3), ('ig_mine', 2), ('done', 1), ('back', 2),
-    ('ig_mine', 3), ('back', 3), ('done', 2), ('done', 3),
+    ('relay2', 1, 0), ('relay3', 0, 0), ('pass1', 0, 0), ('relay2', 1, 2), ('relay1', 2, 0),
+    ('relay1', 2, 1), ('start', 3, 0), ('pass2', 0, 0), ('relay3', 1, 2), ('pass1', 1, 2),
+    ('relay2', 2, 1), ('forward', 0), ('relay2', 2, 0), ('grad', 0, 0), ('pass2', 1, 2),
+    ('grad', 0, 1), ('relay3', 2, 1), ('grad', 0, 2), ('relay1', 3, 0), ('grad', 0, 3),
+    ('x1a', 0, 0), ('forward', 1), ('rs_x2', 0, 1), ('x1b', 0, 0), ('relay2', 3, 0),
+    ('grad', 1, 0), ('rs_x2', 0, 0), ('grad', 1, 1), ('relay3', 3, 0), ('grad', 1, 2),
+    ('pass1', 3, 0), ('x3', 0, 1), ('grad', 1, 3), ('x1a', 1, 0), ('rs_x2', 1, 1),
+    ('forward', 2), ('grad', 2, 0), ('rs_z', 0), ('pass2', 3, 0), ('grad', 2, 1),
+    ('grad', 2, 2), ('x1b', 1, 0), ('rs_x2', 1, 0), ('x3', 1, 1), ('rs_yh', 0),
+    ('x1a', 2, 0), ('grad', 2, 3), ('rs_x2', 2, 1), ('forward', 3), ('grad', 3, 0),
+    ('back', 0), ('rs_z', 1), ('grad', 3, 1), ('x1b', 2, 0), ('rs_x2', 2, 0),
+    ('grad', 3, 2), ('done', 0), ('x1a', 3, 0), ('x3', 2, 1), ('grad', 3, 3),
+    ('rs_x2', 3, 1), ('ig_theirs', 0), ('rs_yh', 1), ('ig_theirs', 1), ('ig_theirs', 2),
+    ('rs_z', 2), ('x1b', 3, 0), ('rs_x2', 3, 0), ('back', 1), ('ig_theirs', 3),
+    ('x3', 3, 1), ('ig_mine', 0), ('rs_yh', 2), ('ig_mine', 1), ('rs_z', 3),
+    ('done', 1), ('ig_mine', 2), ('back', 2), ('ig_mine', 3), ('back', 3),
+    ('done', 2), ('done', 3),
 )
 
 WIDTHS = tuple(128 if half else 256 for _, half in CHUNKS)
 NCHUNK = len(CHUNKS)
-N_IN, N_OUT = 88, 14
+N_IN, N_OUT = 89, 14
 
 
 def adamw(master, moment_first, moment_second, grad):

time: 104 us -> 101 us (0.971)
  Pallas kernels: 95 us -> 92.2 us
    pallas_call x1, Pallas kernels: 95 us -> 92.2 us  [fused(): pl.pallas_call(kernel, out_shape=[jax.ShapeDtypeStruct((TOK, D), bf16), j...]
where the time goes in v5:
time: 101 us
  Pallas kernels  92.2 us (91%)
  other arithmetic  6.41 us (6%)
  local copies, waits for them, and re-layouts  2.02 us (2%)
    pallas_call x1, Pallas kernels, fused(): pl.pallas_call(kernel, out_shape=[jax.ShapeDtypeStruct((TOK, D), bf16), j...  92.2 us
    sub x1, other arithmetic, adamw(): return (master - 0.01 * update, first_next, second_next)  6.41 us

profile of v5, /device:TPU:1, one launch (start us, length us, event | category | flops | bytes accessed | tf_op | source)
XLA Modules:
  0.0 101.3 jit_solution(12614387567095164535)
XLA Ops:
  0.6 92.2 %shard_map.84 = (bf16[512,4096]{1,0:T(8,128)(2,1)}, bf16[256,1792]{1,0:T(8,128)(2,1)}) custom-call(bf16[512,4096]{1,0:T(8,128)(2,1)} %tokens.1, bf16[512,896]{1,0:T(8,128)(2,1)} %hidden.1, f32[256,1792]{1,0:T(8,128)} %master.1), custom_call_target="tpu_custom_call" | custom-call | flops 22499999744 | bytes 20000000 | tf_op jit(solution)/shard_map/pallas_call | solution.py:589
  92.8 0.0 copy-start
  92.8 6.4 %multiply_subtract_fusion = (f32[256,1792]{1,0:T(8,128)}, f32[256,1792]{1,0:T(8,128)}, f32[256,1792]{1,0:T(8,128)}) fusion(f32[256,1792]{1,0:T(8,128)} %master.1, bf16[256,1792]{1,0:T(8,128)(2,1)} %get-tuple-element.7, f32[256,1792]{1,0:T(8,128)} %param.8, f32[256,1792]{1,0:T(8,128)} %param.9), kind=kLoop, calls=%fused_computation.4 | loop fusion | flops 7340032 | bytes 11927552 | tf_op jit(solution)/shard_map/sub | solution.py:57
  99.2 0.0 copy-done
  99.3 2.0 %copy.10 = bf16[512,4096]{1,0:T(8,128)(2,1)} copy(bf16[512,4096]{1,0:T(8,128)(2,1)S(1)} %copy-done) | data formatting | bytes 8388608
Async XLA Ops:
  92.8 6.4 %copy-start = (bf16[512,4096]{1,0:T(8,128)(2,1)S(1)}, bf16[512,4096]{1,0:T(8,128)(2,1)}, u32[]{:S(2)}) copy-start(bf16[512,4096]{1,0:T(8,128)(2,1)} %get-tuple-element.15) | copy-start | bytes 12582916

commit v6 on v5

--- a/solution.py
+++ b/solution.py
@@ -336,7 +336,7 @@
         block = CHUNKS[k][0]
         at = (1 - c) * 384 if block == 3 else (c + block) * 128
 
-        @pl.loop(0, 2)
+        @pl.loop(0, 2, unroll=True)
         def _(i):
             rows = pl.ds(pl.multiple_of(i * 512, 512), 512)
             gu = jnp.dot(tok[rows, :], w[k][...].reshape(D, n), preferred_element_type=f32) * MULT

time: 101 us -> 101 us (level)
  no operation moved by 1% of the time
where the time goes in v6:
time: 101 us
  Pallas kernels  91.7 us (91%)
  other arithmetic  6.41 us (6%)
  local copies, waits for them, and re-layouts  2.02 us (2%)
    pallas_call x1, Pallas kernels, fused(): pl.pallas_call(kernel, out_shape=[jax.ShapeDtypeStruct((TOK, D), bf16), j...  91.7 us
    sub x1, other arithmetic, adamw(): return (master - 0.01 * update, first_next, second_next)  6.41 us

profile of v6, /device:TPU:1, one launch (start us, length us, event | category | flops | bytes accessed | tf_op | source)
XLA Modules:
  0.0 100.7 jit_solution(4494097828084680198)
XLA Ops:
  0.6 91.7 %shard_map.84 = (bf16[512,4096]{1,0:T(8,128)(2,1)}, bf16[256,1792]{1,0:T(8,128)(2,1)}) custom-call(bf16[512,4096]{1,0:T(8,128)(2,1)} %tokens.1, bf16[512,896]{1,0:T(8,128)(2,1)} %hidden.1, f32[256,1792]{1,0:T(8,128)} %master.1), custom_call_target="tpu_custom_call" | custom-call | flops 22499999744 | bytes 20000000 | tf_op jit(solution)/shard_map/pallas_call | solution.py:589
  92.3 0.0 copy-start
  92.3 6.4 %multiply_subtract_fusion = (f32[256,1792]{1,0:T(8,128)}, f32[256,1792]{1,0:T(8,128)}, f32[256,1792]{1,0:T(8,128)}) fusion(f32[256,1792]{1,0:T(8,128)} %master.1, bf16[256,1792]{1,0:T(8,128)(2,1)} %get-tuple-element.7, f32[256,1792]{1,0:T(8,128)} %param.8, f32[256,1792]{1,0:T(8,128)} %param.9), kind=kLoop, calls=%fused_computation.4 | loop fusion | flops 7340032 | bytes 11927552 | tf_op jit(solution)/shard_map/sub | solution.py:57
  98.7 0.0 copy-done
  98.7 2.0 %copy.10 = bf16[512,4096]{1,0:T(8,128)(2,1)} copy(bf16[512,4096]{1,0:T(8,128)(2,1)S(1)} %copy-done) | data formatting | bytes 8388608
Async XLA Ops:
  92.3 6.4 %copy-start = (bf16[512,4096]{1,0:T(8,128)(2,1)S(1)}, bf16[512,4096]{1,0:T(8,128)(2,1)}, u32[]{:S(2)}) copy-start(bf16[512,4096]{1,0:T(8,128)(2,1)} %get-tuple-element.15) | copy-start | bytes 12582916
